TPU v7x, 512 devices: a whole 4x8x8 slice. The times are simulated.
512 devices in a mesh: seq: 128 (over z, y, core), mp: 4 (over x).
Axes of the slice: x: 4, y: 8, z: 8, core: 2. Of those that a mesh axis runs over, the one named last changes fastest.
Arguments:
- byte_hidden: bfloat16 [131072, 1024], P('seq', 'mp'), may hold values from -24 to 24
- patch_start: int32 [131072], P('seq'), may hold values from 0 to 1, as said below
- pool_query: bfloat16 [1024], P('mp'), may hold values from -4 to 4
- in_weight: bfloat16 [1024, 4096], P('seq', 'mp'), may hold values from -0.1875 to 0.1875
- latent_grad: bfloat16 [65536, 4096], P('seq', 'mp'), may hold values from -6 to 6
Outputs:
- latent: bfloat16 [65536, 4096], P('seq', 'mp')
- grad_weight: float32 [1024, 4096], P('seq', 'mp')
- grad_bytes: bfloat16 [131072, 1024], P('seq', 'mp')
Inputs may be any that keep to these rules, and one draw needn't show every extreme that they name: `patch_start`: byte 0 begins a patch, and so does every byte whose position is 16 // 2 modulo 16; of the bytes 2k and 2k+1 at most one begins a patch. So no patch is longer than 16 bytes, and some patch is exactly 16 long. Each aligned block of 1024 bytes holds at most 512 patch starts, and one block holds exactly 512.
All inputs are finite; a program needn't handle non-finite values.
Results may differ from a plain program's by a relative error of at most 0.0049.
Values may be sent and summed in bfloat16 or wider, within the bound.
A program may use at most 64 MiB of HBM per device.

v0:
```python
import math

import jax
import jax.numpy as jnp
from jax import lax
from jax.sharding import PartitionSpec as P

HEAD_DIM = 64
MAXLEN = 16


soft_cap = 20.0


def from_behind(value, axis, steps):
    count = lax.axis_size(axis)
    leading, last = (max(0, -steps), min(count, count - steps))
    return lax.ppermute(value, axis, [(source, source + steps) for source in range(leading, last)])


def shards(byte_hidden, patch_start, pool_query, in_weight, latent_grad):
    rows_local, feats = byte_hidden.shape
    slots = latent_grad.shape[0]
    head_dim = HEAD_DIM
    local_heads = feats // head_dim
    inv_root = 1.0 / math.sqrt(head_dim)
    query = pool_query.astype(jnp.float32)

    def capped_scores(block):
        raw = (block.astype(jnp.float32) * query).reshape(-1, local_heads, head_dim).sum(
            -1
        ) * inv_root
        return soft_cap * jnp.tanh(raw / soft_cap)

    capped = capped_scores(byte_hidden)
    weight_exp = jnp.exp(capped)
    hidden_f = byte_hidden.astype(jnp.float32)
    patch_total = jnp.sum(patch_start)
    segment = jnp.cumsum(patch_start) - 1
    leading = segment < 0
    inside = jnp.maximum(segment, 0)
    keep_own = jnp.where(leading, 0.0, 1.0).astype(jnp.float32)[:, None]
    weighted = jnp.repeat(weight_exp, head_dim, axis=1) * hidden_f
    numer = jax.ops.segment_sum(weighted * keep_own, inside, num_segments=slots)
    denom = jax.ops.segment_sum(weight_exp * keep_own, inside, num_segments=slots)
    lead_mask = leading[:MAXLEN].astype(jnp.bfloat16)
    next_rows, next_mask = from_behind((byte_hidden[:MAXLEN], lead_mask), "seq", -1)
    next_exp = jnp.exp(capped_scores(next_rows)) * next_mask.astype(jnp.float32)[:, None]
    recv_num = jnp.sum(
        jnp.repeat(next_exp, head_dim, axis=1) * next_rows.astype(jnp.float32), axis=0
    )
    recv_den = jnp.sum(next_exp, axis=0)
    slot_index = jnp.arange(slots)
    last_row = (slot_index == patch_total - 1).astype(jnp.float32)[:, None]
    numer = numer + last_row * recv_num
    denom = denom + last_row * recv_den
    live = (slot_index < patch_total)[:, None]
    safe = jnp.where(live, denom, jnp.float32(1.0))
    pooled = jnp.where(live, numer / jnp.repeat(safe, head_dim, axis=1), jnp.float32(0.0))
    pooled_low = pooled.astype(jnp.bfloat16)
    pooled_full = lax.all_gather(pooled_low, "mp", axis=1, tiled=True)
    weight_full = lax.all_gather(in_weight, "seq", axis=0, tiled=True)
    latent = jnp.dot(pooled_full, weight_full, preferred_element_type=jnp.float32)
    partial_value = lax.dot_general(
        latent_grad, weight_full, (((1,), (1,)), ((), ())), preferred_element_type=jnp.float32
    )
    latent_out = latent.astype(jnp.bfloat16)
    received = lax.all_to_all(
        partial_value.astype(jnp.bfloat16), "mp", split_axis=1, concat_axis=0, tiled=True
    )
    grad_pooled = received.reshape(-1, slots, feats).astype(jnp.float32).sum(0)
    grad_scale = 1.0 / math.sqrt(lax.axis_size("seq") * slots)
    grad_weight = lax.psum_scatter(
        lax.dot_general(
            pooled_full, latent_grad, (((0,), (0,)), ((), ())), preferred_element_type=jnp.float32
        )
        * grad_scale,
        "seq",
        scatter_dimension=0,
        tiled=True,
    )
    last_grad = jnp.sum(last_row * grad_pooled, axis=0)
    last_pooled = jnp.sum(last_row * pooled, axis=0)
    last_den = jnp.sum(last_row * safe, axis=0)
    prev_grad, prev_pooled, prev_den = from_behind((last_grad, last_pooled, last_den), "seq", 1)
    lead_col = leading[:, None]
    grad_rows = jnp.where(lead_col, prev_grad[None, :], jnp.take(grad_pooled, inside, axis=0))
    pooled_rows = jnp.where(lead_col, prev_pooled[None, :], jnp.take(pooled, inside, axis=0))
    den_rows = jnp.where(lead_col, prev_den[None, :], jnp.take(safe, inside, axis=0))
    share = weight_exp / den_rows
    inner = (
        (grad_rows * (hidden_f - pooled_rows)).reshape(rows_local, local_heads, head_dim).sum(-1)
    )
    coeff = share * inner * (1.0 - (capped / soft_cap) ** 2) * inv_root
    grad_bytes = (
        jnp.repeat(share, head_dim, axis=1) * grad_rows
        + jnp.repeat(coeff, head_dim, axis=1) * query
    )
    return (latent_out, grad_weight, grad_bytes.astype(jnp.bfloat16))


def solution(mesh):
    in_specs = (P("seq", "mp"), P("seq"), P("mp"), P("seq", "mp"), P("seq", "mp"))
    out_specs = (P("seq", "mp"), P("seq", "mp"), P("seq", "mp"))
    return jax.shard_map(shards, mesh=mesh, in_specs=in_specs, out_specs=out_specs, check_vma=False)
```

profile of v0, /device:TPU:1, one launch (start us, length us, event | category | flops | bytes accessed | tf_op | source)
XLA Modules:
  0.0 368.9 jit_solution(7244079275878472114)
XLA Ops:
  7.2 0.0 copy-start
  7.2 0.0 all-gather.5.cloned.1.call-start
  7.2 0.7 all-gather.5.cloned.1.call-update
  7.9 1.0 reduce-window.9
  8.9 0.1 slice.14
  9.0 0.1 slice_reduce_fusion
  9.1 0.1 broadcast_select_fusion.1
  9.2 8.8 %collective-permute-start.1 = (bf16[16]{0:T(256)(128)(2,1)S(1)}, bf16[16]{0:T(256)(128)(2,1)S(1)}, u32[]{:S(2)}, u32[]{:S(2)}) collective-permute-start(bf16[16]{0:T(256)(128)(2,1)S(1)} %slice_convert_fusion), channel_id=1, source_target_pairs={{4,0},{8,4},{12,8},{16,12},{20,16},{24,20},{28,24},{32,28},{36,32}... | collective-permute-start | bytes 104 | tf_op jit(solution)/shard_map/ppermute | solution.py:18
  18.0 0.7 slice.13
  18.7 1.9 collective-permute-start
  20.6 1.3 reduce_sum.90
  21.9 0.7 convert_element_type.42
  22.6 1.1 convert_multiply_fusion.1
  23.7 0.3 copy.41
  24.7 0.1 bitcast_reduce_fusion.1
  24.8 0.1 compare_and_fusion
  24.9 0.7 iota_compare_fusion.1
  25.5 1.0 copy.43
  26.6 0.1 broadcast_in_dim.125
  26.7 0.3 copy.42
  27.1 0.1 reshape.128
  27.2 0.1 reduce_sum.91
  27.3 0.1 fusion.8
  27.3 0.1 broadcast_in_dim.124
  27.4 0.1 reshape.131
  27.5 72.4 %all-gather.5.cloned.1.call-done = bf16[1024,1024]{1,0:T(8,128)(2,1)} async-done(((bf16[8,1024]{1,0:T(8,128)(2,1)}), bf16[1024,1024]{1,0:T(8,128)(2,1)}) %all-gather.5.cloned.1.call-update) | async-done | bytes 2097168 | tf_op jit(solution)/shard_map/all_gather | solution.py:62
  100.0 2.9 convolution_convert_fusion
  102.8 1.0 copy.53
  103.9 4.2 %all-to-all-start = ((bf16[512,4,256]{2,0,1:T(8,128)(2,1)}), bf16[512,4,256]{2,0,1:T(8,128)(2,1)}, u32[]{:S(2)}, u32[]{:S(2)}) async-start(bf16[512,4,256]{2,0,1:T(8,128)(2,1)} %bitcast.24), calls=%async_computation.1 | async-start | bytes 2097152 | tf_op jit(solution)/shard_map/all_to_all | solution.py:68
  108.1 0.0 all-gather.3.cloned.1.call-start
  108.2 0.1 broadcast_multiply_fusion.1
  108.3 6.9 %scatter_fusion = f32[512,4]{1,0:T(8,128)S(1)} fusion(f32[512,4]{1,0:T(8,128)S(1)} %broadcast_multiply_fusion.1, s32[1024]{0:T(1024)S(1)} %get-tuple-element.9, f32[1024,4]{1,0:T(8,128)S(1)} %copy-done.3), kind=kCustom, calls=%fused_computation.4 | custom fusion | flops 4096 | bytes 53248 | tf_op jit(solution)/shard_map/scatter-add | solution.py:45
  115.3 0.2 multiply_reduce_fusion.2
  115.5 0.1 copy.44
  115.6 0.9 broadcast_in_dim.130
  116.5 1.2 copy.45
  117.7 0.9 broadcast_multiply_fusion
  118.7 9.1 %scatter_custom_fusion = f32[512,256]{1,0:T(8,128)} fusion(f32[512,256]{1,0:T(8,128)} %broadcast_multiply_fusion, s32[1024]{0:T(1024)S(1)} %get-tuple-element.9, f32[1024,256]{1,0:T(8,128)S(1)} %copy.42, bf16[1024,256]{1,0:T(8,128)(2,1)S(1)} %copy-done.1, f32[1024]{0:T(1024)S(1)} %get-tuple-element.15), kind=kCustom, calls=%fused_computation.13 | custom fusion | flops 1048576 | bytes 2101248 | tf_op jit(solution)/shard_map/scatter-add | solution.py:44
  127.8 1.4 convert_reduce_fusion
  129.2 1.3 multiply_reduce_fusion.1
  130.5 0.7 convert_element_type.46
  131.2 0.0 all-gather.3.cloned.1.call-update
  131.2 0.0 reduce-scatter.2.cloned.1.call-start
  131.3 27.5 %all-gather.3.cloned.1.call-done = bf16[512,1024]{1,0:T(8,128)(2,1)} async-done(((bf16[512,256]{1,0:T(8,128)(2,1)}), bf16[512,1024]{1,0:T(8,128)(2,1)}) %all-gather.3.cloned.1.call-update) | async-done | bytes 1048592 | tf_op jit(solution)/shard_map/all_gather | solution.py:61
  158.8 4.4 %convolution_multiply_fusion = f32[1024,1024]{1,0:T(8,128)} fusion(bf16[512,1024]{1,0:T(8,128)(2,1)} %all-gather.3.cloned.1.call-done, bf16[512,1024]{1,0:T(8,128)(2,1)S(1)} %copy-done), kind=kOutput, calls=%fused_computation.5 | convolution fusion | flops 1074790400 | bytes 6291456 | tf_op jit(solution)/shard_map/dot_general | solution.py:74
  163.3 0.0 reduce-scatter.2.cloned.1.call-update
  163.3 4.5 %collective-permute-start.3 = (f32[256]{0:T(256)S(1)}, f32[256]{0:T(256)S(1)}, u32[]{:S(2)}, u32[]{:S(2)}) collective-permute-start(f32[256]{0:T(256)S(1)} %get-tuple-element.4), channel_id=1, source_target_pairs={{0,4},{4,8},{8,12},{12,16},{16,20},{20,24},{24,28},{28,32},{32,36}... | collective-permute-start | bytes 3080 | tf_op jit(solution)/shard_map/ppermute | solution.py:18
  167.8 1.9 collective-permute-start.4
  169.8 3.7 collective-permute-start.2
  173.5 2.8 gather_fusion
  176.3 0.2 copy.46
  176.5 3.5 gather_fusion.1
  180.0 4.7 %gather_fusion.2 = f32[1024,256]{1,0:T(8,128)} fusion(f32[512,256]{1,0:T(8,128)S(1)} %get-tuple-element.10, s32[1024]{0:T(1024)S(1)} %get-tuple-element.20), kind=kCustom, calls=%fused_computation.1.clone | custom fusion | bytes 2101248 | tf_op jit(solution)/shard_map/jit(_take)/gather | solution.py:88
  184.7 2.8 fusion.3
  187.4 1.6 copy.49
  189.0 0.1 bitcast_reduce_fusion
  189.1 0.1 multiply_multiply_fusion
  189.2 0.1 broadcast_in_dim.140
  189.3 1.3 copy.50
  190.6 0.1 broadcast_in_dim.136
  190.7 1.3 copy.48
  192.1 2.9 add_convert_fusion
  195.0 2.2 convolution_convert_fusion.1
  197.2 165.2 %reduce-scatter.2.cloned.1.call-done = f32[8,1024]{1,0:T(8,128)} async-done(((f32[1024,1024]{1,0:T(8,128)}), f32[8,1024]{1,0:T(8,128)}) %reduce-scatter.2.cloned.1.call-update) | async-done | bytes 32784 | tf_op jit(solution)/shard_map/reduce_scatter | solution.py:73
  (26 shorter events, 0.1 us)
Async XLA Ops:
  7.2 92.8 %copy-start = (bf16[512,1024]{1,0:T(8,128)(2,1)S(1)}, bf16[512,1024]{1,0:T(8,128)(2,1)}, u32[]{:S(2)}) copy-start(bf16[512,1024]{1,0:T(8,128)(2,1)} %param.11) | copy-start | bytes 3145732
  7.2 92.8 %all-gather.5.cloned.1.call-start = ((), (), s32[]{:S(2)}) async-start(), calls=%async_computation.3 | async-start | bytes 2113536 | tf_op jit(solution)/shard_map/all_gather | solution.py:62
  9.2 17.8 %collective-permute-start.1 = (bf16[16]{0:T(256)(128)(2,1)S(1)}, bf16[16]{0:T(256)(128)(2,1)S(1)}, u32[]{:S(2)}, u32[]{:S(2)}) collective-permute-start(bf16[16]{0:T(256)(128)(2,1)S(1)} %slice_convert_fusion), channel_id=1, source_target_pairs={{4,0},{8,4},{12,8},{16,12},{20,16},{24,20},{28,24},{32,28},{36,32}... | collective-permute-start | bytes 104 | tf_op jit(solution)/shard_map/ppermute | solution.py:18
  18.7 8.4 %collective-permute-start = (bf16[16,256]{1,0:T(8,128)(2,1)S(1)}, bf16[16,256]{1,0:T(8,128)(2,1)S(1)}, u32[]{:S(2)}, u32[]{:S(2)}) collective-permute-start(bf16[16,256]{1,0:T(8,128)(2,1)S(1)} %slice.13), channel_id=1, source_target_pairs={{4,0},{8,4},{12,8},{16,12},{20,16},{24,20},{28,24},{32,28},{36,32}... | collective-permute-start | bytes 24584 | tf_op jit(solution)/shard_map/ppermute | solution.py:18
  102.8 5.5 %copy-start.3 = (f32[1024,4]{1,0:T(8,128)S(1)}, f32[1024,4]{1,0:T(8,128)}, u32[]{:S(2)}) copy-start(f32[1024,4]{1,0:T(8,128)} %copy.43) | copy-start | bytes 49156
  103.9 23.9 %all-to-all-start = ((bf16[512,4,256]{2,0,1:T(8,128)(2,1)}), bf16[512,4,256]{2,0,1:T(8,128)(2,1)}, u32[]{:S(2)}, u32[]{:S(2)}) async-start(bf16[512,4,256]{2,0,1:T(8,128)(2,1)} %bitcast.24), calls=%async_computation.1 | async-start | bytes 2097152 | tf_op jit(solution)/shard_map/all_to_all | solution.py:68
  108.1 50.7 %all-gather.3.cloned.1.call-start = ((), (), s32[]{:S(2)}) async-start(), calls=%async_computation.2 | async-start | bytes 1310720 | tf_op jit(solution)/shard_map/all_gather | solution.py:61
  115.3 3.4 copy-start.1
  131.2 231.1 %reduce-scatter.2.cloned.1.call-start = ((), (), s32[]{:S(2)}) async-start(), calls=%async_computation.4 | async-start | bytes 4227072 | tf_op jit(solution)/shard_map/reduce_scatter | solution.py:73
  163.3 21.4 %collective-permute-start.3 = (f32[256]{0:T(256)S(1)}, f32[256]{0:T(256)S(1)}, u32[]{:S(2)}, u32[]{:S(2)}) collective-permute-start(f32[256]{0:T(256)S(1)} %get-tuple-element.4), channel_id=1, source_target_pairs={{0,4},{4,8},{8,12},{12,16},{16,20},{20,24},{24,28},{28,32},{32,36}... | collective-permute-start | bytes 3080 | tf_op jit(solution)/shard_map/ppermute | solution.py:18
  167.8 16.8 %collective-permute-start.4 = (f32[256]{0:T(256)S(1)}, f32[256]{0:T(256)S(1)}, u32[]{:S(2)}, u32[]{:S(2)}) collective-permute-start(f32[256]{0:T(256)S(1)} %get-tuple-element.5), channel_id=1, source_target_pairs={{0,4},{4,8},{8,12},{12,16},{16,20},{20,24},{24,28},{28,32},{32,36}... | collective-permute-start | bytes 3080 | tf_op jit(solution)/shard_map/ppermute | solution.py:18
  169.8 19.3 %collective-permute-start.2 = (f32[4]{0:T(128)S(1)}, f32[4]{0:T(128)S(1)}, u32[]{:S(2)}, u32[]{:S(2)}) collective-permute-start(f32[4]{0:T(128)S(1)} %get-tuple-element.11), channel_id=1, source_target_pairs={{0,4},{4,8},{8,12},{12,16},{16,20},{20,24},{24,28},{28,32},{32,36}... | collective-permute-start | bytes 56 | tf_op jit(solution)/shard_map/ppermute | solution.py:18
  180.0 4.7 %copy-start.2 = (bf16[1024,256]{1,0:T(8,128)(2,1)S(1)}, bf16[1024,256]{1,0:T(8,128)(2,1)}, u32[]{:S(2)}) copy-start(bf16[1024,256]{1,0:T(8,128)(2,1)} %param.7) | copy-start | bytes 1572868
  192.0 2.9 copy-start.4
  192.1 2.9 copy-start.5
Sparse Core Ops, SparseCore 0:
  11.1 88.7 all-gather.4
  131.4 27.4 all-gather.2
  163.8 198.5 reduce-scatter.1
where the time goes:
time: 374 us; the launch traced here: 369 us
  waiting for transfers between devices  266 us (71%)
  other arithmetic  31.8 us (9%)
  starting transfers between devices  25.2 us (7%)
  local copies, waits for them, and re-layouts  21.8 us (6%)
  between operations  14.7 us (4%)
  matrix products  9.55 us (3%)
    reduce_scatter x1, waiting for transfers between devices, shards(): lax.psum_scatter(lax.dot_general(pooled_full, latent_grad, (((0,), (0,)),...  165 us
    all_gather x1, waiting for transfers between devices, shards(): weight_full = lax.all_gather(in_weight, 'seq', axis=0, tiled=True)  72.4 us
    all_gather x1, waiting for transfers between devices, shards(): pooled_full = lax.all_gather(pooled_low, 'mp', axis=1, tiled=True)  27.5 us
    ppermute x5, starting transfers between devices, from_behind(): lax.ppermute(value, axis, [(source, source + steps) for source in range(l...  20.8 us
    scatter-add x1, other arithmetic, shards(): numer = jax.ops.segment_sum(weighted * keep_own, inside, num_segments=slots)  9.13 us
  transfers between devices with their start and end apart: 9, of which 3 were waited for; matrix products, arithmetic and copies ran while one was open for 14% of the time, Pallas kernels for 0%

commit v1 on v0

v1 whole, which is shorter than its diff:
```python
import functools
import math

import jax
import jax.numpy as jnp
from jax import lax
from jax.experimental import pallas as pl
from jax.experimental.pallas import tpu as pltpu
from jax.sharding import PartitionSpec as P

HEAD_DIM = 64
SOFT_CAP = 20.0
RING = 8
F32 = jnp.float32
BF16 = jnp.bfloat16

W_PAIR, H_NEXT, H_PREV, S_NEXT, S_PREV, G_NEXT, G_PAIR = range(7)
A1A, A1B, A2A, A2B = 7, 14, 21, 28
WPA, WPB = 35, 43
X_UP0, X_UP1, X_UPF, X_DN1, X_DN0, X_DNF = range(51, 57)
PF_PAIR = 57
C_UPR, C_UPD, C_UPS, C_DNR, C_DND, C_DNS = range(65, 71)
D1A, D1B, D2A, D2B = 71, 78, 85, 92
F_PAIR = 99
SLOTS_SEM = 100


def dot(a, b):
    return jnp.dot(a, b, preferred_element_type=F32)


def dot_nt(a, b):
    return lax.dot_general(a, b, (((1,), (1,)), ((), ())), preferred_element_type=F32)


def dot_tn(a, b):
    return lax.dot_general(a, b, (((0,), (0,)), ((), ())), preferred_element_type=F32)


def split(value):
    high = value.astype(BF16)
    return high, (value - high.astype(F32)).astype(BF16)


def iota(shape, dim):
    return lax.broadcasted_iota(jnp.int32, shape, dim)


def kernel(
    h_hbm, st_ref, q_ref, w_ref, g_hbm,
    lat_hbm, gw_ref, gb_hbm,
    hx, st8, st_n, st_p, w32, w32r, wg, wq, gx, gl_send, gc,
    hot, hot_t, xs, ws, ts, pool, den, yv, share_s, diff_s, coef_s,
    pf, part, cr_up, cr_dn, cs_up, cs_dn, c_up, c_dn, zv, lat, gb,
    sa, sb, ra, rb, ta, tb, ua, ub, fin_s, fin_r,
    loc, ss, rs,
):
    s = lax.axis_index("seq")
    a = lax.axis_index("mp")
    n_seq, n_mp = lax.axis_size("seq"), lax.axis_size("mp")
    slots = g_hbm.shape[0]
    rows = h_hbm.shape[0]
    feats = h_hbm.shape[1]
    c = lax.rem(s, 2)
    y = lax.rem(lax.div(s, 2), RING)
    z = lax.div(s, 2 * RING)

    def wrap(value, size):
        return lax.rem(value + size, size)

    pair = (s + 1 - 2 * c, a)
    nxt = (wrap(s + 1, n_seq), a)
    prv = (wrap(s - 1, n_seq), a)
    up = (s, wrap(a + 1, n_mp))
    dn = (s, wrap(a - 1, n_mp))
    a_up, a_dn, a_far = wrap(a + 1, n_mp), wrap(a - 1, n_mp), wrap(a + 2, n_mp)

    def y_at(k):
        return wrap(y + k, RING)

    def z_at(k):
        return wrap(z + k, RING)

    def dev_y(k):
        return ((z * RING + y_at(k)) * 2 + c, a)

    def dev_z(k):
        return ((z_at(k) * RING + y) * 2 + c, a)

    def remote(src, dst, slot, device):
        return pltpu.make_async_remote_copy(
            src_ref=src, dst_ref=dst, send_sem=ss.at[slot], recv_sem=rs.at[slot],
            device_id=device, device_id_type=pl.DeviceIdType.MESH,
        )

    def send(src, dst, slot, device):
        remote(src, dst, slot, device).start()

    def arrived(dst, slot):
        remote(dst, dst, slot, pair).wait_recv()

    def sent(src, slot):
        remote(src, src, slot, pair).wait_send()

    barrier = pltpu.get_barrier_semaphore()

    def greet(device):
        pl.semaphore_signal(barrier, inc=1, device_id=device, device_id_type=pl.DeviceIdType.MESH)

    for device in (pair, nxt, prv, up, dn):
        greet(device)

    def greet_ring(k, carry):
        greet(dev_y(k))
        greet(dev_z(k))
        return carry

    lax.fori_loop(1, RING, greet_ring, 0)

    own_cols = pl.ds(pl.multiple_of(c * 512, 512), 512)
    pair_cols = pl.ds(pl.multiple_of((1 - c) * 512, 512), 512)
    copy_h = pltpu.make_async_copy(h_hbm, hx.at[pl.ds(0, rows)], loc.at[0])
    copy_h.start()
    copy_g = pltpu.make_async_copy(g_hbm, gx.at[pl.ds(0, slots)], loc.at[1])
    copy_g.start()
    copy_gc = pltpu.make_async_copy(g_hbm.at[:, own_cols], gc.at[0], loc.at[2])
    copy_gc.start()

    w32[...] = w_ref[...].astype(F32)
    st_row = st_ref[...].astype(F32)
    st8[...] = jnp.broadcast_to(st_row, st8.shape)
    hx[rows + 16:rows + 112, :] = jnp.zeros((96, feats), BF16)

    pl.semaphore_wait(barrier, 5 + 2 * (RING - 1))

    send(w32, w32r, W_PAIR, pair)
    send(h_hbm.at[pl.ds(rows - 16, 16)], hx.at[pl.ds(rows + 112, 16)], H_NEXT, nxt)
    send(h_hbm.at[pl.ds(0, 16)], hx.at[pl.ds(rows, 16)], H_PREV, prv)
    send(st8.at[:, pl.ds(rows - 128, 128)], st_p, S_NEXT, nxt)
    send(st8.at[:, pl.ds(0, 128)], st_n, S_PREV, prv)
    send(g_hbm.at[:, pair_cols], gc.at[1], G_PAIR, pair)

    r128, c128 = iota((128, 128), 0), iota((128, 128), 1)
    upper = jnp.where(r128 <= c128, 1.0, 0.0).astype(BF16)
    lower = jnp.where(c128 <= r128, 1.0, 0.0).astype(BF16)
    ones = jnp.ones((128, 128), BF16)
    hot_rows = hot.shape[0]
    slot_col = iota((hot_rows, 128), 0).astype(F32)
    lane = iota((128, 128), 1).astype(F32)
    total = jnp.zeros((8, 128), F32)
    lead8 = None
    for k in range(rows // 128):
        st_k = st8[:, 128 * k:128 * k + 128].astype(BF16)
        row_id = total + dot(st_k, upper) - 1.0
        row_id = jnp.where(row_id < 0.0, F32(slots), row_id)
        hot[:, 128 * k:128 * k + 128] = jnp.where(slot_col == row_id[0:1], 1.0, 0.0).astype(BF16)
        st_t = jnp.broadcast_to(st8[0:1, 128 * k:128 * k + 128], (128, 128)).astype(BF16)
        col_id = dot_nt(lower, st_t) + total[0:1] - 1.0
        if k == 0:
            lead8 = jnp.where(col_id[0:8] < 0.0, 1.0, 0.0).astype(F32)
        for j in range(slots // 128):
            hot_t[128 * k:128 * k + 128, 128 * j:128 * j + 128] = jnp.where(
                col_id == lane + 128.0 * j, 1.0, 0.0
            ).astype(BF16)
        total = total + dot(st_k, ones)
    lead8 = jnp.concatenate([lead8, lead8], axis=1)

    arrived(w32r, W_PAIR)
    w_own, w_other = w32[...], w32r[...]
    first = c == 0
    w16 = jnp.concatenate(
        [jnp.where(first, w_own, w_other), jnp.where(first, w_other, w_own)], axis=0
    )
    w_half = jnp.where(first, w16[:, :512], w16[:, 512:]).astype(BF16)
    wg[c, 0, z, y] = w_half[:, :256]
    wg[c, 1, y, z] = w_half[:, 256:]

    def lines(k, carry):
        send(wg.at[c, 0, z, y], wg.at[c, 0, z, y], A1A + k - 1, dev_y(k))
        send(wg.at[c, 1, y, z], wg.at[c, 1, y, z], A1B + k - 1, dev_z(k))
        return carry

    lax.fori_loop(1, RING, lines, 0)

    same = lax.div(iota((feats, feats), 0), HEAD_DIM) == lax.div(iota((feats, feats), 1), HEAD_DIM)
    query = q_ref[...].astype(F32)
    q_mat = jnp.where(same, jnp.broadcast_to(query, (feats, feats)), 0.0).astype(BF16)
    head_ones = jnp.where(same, 1.0, 0.0).astype(BF16)
    inv_root = 1.0 / math.sqrt(HEAD_DIM)

    def score(start, size):
        at = pl.ds(start, size)
        h = hx[at]
        t = jnp.tanh(dot_nt(h, q_mat) * (inv_root / SOFT_CAP))
        w = jnp.exp(SOFT_CAP * t)
        ws[at] = w
        ts[at] = t
        xs[at, 0:256], xs[at, 256:512] = split(w * h.astype(F32))
        xs[at, 512:768], xs[at, 768:1024] = split(w)

    copy_h.wait()

    def score_own(i, carry):
        score(pl.multiple_of(i * 256, 256), 256)
        return carry

    lax.fori_loop(0, rows // 256, score_own, 0)

    def planes(k, carry):
        arrived(wg.at[c, 0, z, y], A1A + k - 1)
        arrived(wg.at[c, 1, y, z], A1B + k - 1)
        return carry

    lax.fori_loop(1, RING, planes, 0)

    def planes_send(k, carry):
        send(wg.at[c, 0, z], wg.at[c, 0, z], A2A + k - 1, dev_z(k))
        send(wg.at[c, 1, y], wg.at[c, 1, y], A2B + k - 1, dev_y(k))
        return carry

    lax.fori_loop(1, RING, planes_send, 0)
    send(wg.at[c, 0, z], wg.at[c, 0, z], WPA, pair)
    send(wg.at[c, 1, y], wg.at[c, 1, y], WPB, pair)

    copy_g.wait()
    pick = iota((16, slots), 1).astype(F32) == (total[0:1, 0:1] - 1.0)
    pick = jnp.where(pick & (iota((16, slots), 0) == 0), 1.0, 0.0).astype(BF16)
    gl_send[...] = dot(pick, gx[0:slots, :]).astype(BF16)
    send(gl_send, gx.at[pl.ds(slots, 16)], G_NEXT, nxt)

    arrived(hx.at[pl.ds(rows + 112, 16)], H_NEXT)
    arrived(hx.at[pl.ds(rows, 16)], H_PREV)
    arrived(st_p, S_NEXT)
    arrived(st_n, S_PREV)
    score(rows, 128)
    after = jnp.where((r128 <= c128) & (c128 < 64), 1.0, 0.0).astype(BF16)
    before = jnp.where((r128 > c128) & (c128 >= 64), 1.0, 0.0).astype(BF16)
    starts_n = jnp.where(s == n_seq - 1, 1.0, st_n[...]).astype(BF16)
    starts_p = jnp.where(s == 0, 1.0, st_p[...]).astype(BF16)
    count = dot(starts_n, after) + dot(starts_p, before)
    halo_slot = jnp.where(iota((8, 128), 1) < 64, total - 1.0, F32(slots))
    halo_slot = jnp.where(count == 0.0, halo_slot, -9.0)
    hot[:, rows:rows + 128] = jnp.where(slot_col == halo_slot[0:1], 1.0, 0.0).astype(BF16)

    onehot = hot[...]
    denom = dot(onehot, xs[:, 512:768]) + dot(onehot, xs[:, 768:1024])
    numer = dot(onehot, xs[:, 0:256]) + dot(onehot, xs[:, 256:512])
    live = denom > 0.0
    denom = jnp.where(live, denom, 1.0)
    pooled = jnp.where(live, numer / denom, 0.0)
    half = slots // 2
    pf[0, a, 0] = pooled[:half].astype(BF16)
    pf[0, a, 1] = pooled[half:slots].astype(BF16)
    send(pf.at[0, a, 0], pf.at[0, a, 0], X_UP0, up)
    send(pf.at[0, a, 1], pf.at[0, a, 1], X_DN1, dn)
    send(pf.at[0, a, 1], pf.at[0, a, 1], X_UP1, up)
    send(pf.at[0, a, 0], pf.at[0, a, 0], X_DN0, dn)

    def to_pair(step, index, part_half):
        send(pf.at[0, index, part_half], pf.at[1, index, part_half],
             PF_PAIR + 2 * step + part_half, pair)

    to_pair(0, a, 0)
    to_pair(0, a, 1)

    yv[:, 0:256], yv[:, 256:512] = split(pooled[:slots])
    yv[:, 512:768], yv[:, 768:1024] = split(denom[:slots])
    prev_pool, prev_den = pooled[slots:slots + 1], denom[slots:slots + 1]

    def lead_rows(value8, size):
        return jnp.concatenate([value8, jnp.zeros((size - 8, feats), F32)], axis=0)

    def weigh(at, extra):
        got = dot(hot_t[at], yv[...])
        pool_rows = got[:, 0:256] + got[:, 256:512]
        den_rows = got[:, 512:768] + got[:, 768:1024]
        if extra is not None:
            pool_rows = pool_rows + extra[0]
            den_rows = den_rows + extra[1]
        t = ts[at]
        share = ws[at] / den_rows
        share_s[at] = share
        diff_s[at] = hx[at].astype(F32) - pool_rows
        coef_s[at] = share * (1.0 - t * t) * (query * inv_root)

    weigh(pl.ds(0, 256), (lead_rows(lead8 * prev_pool, 256), lead_rows(lead8 * prev_den, 256)))

    def weigh_more(i, carry):
        weigh(pl.ds(pl.multiple_of(i * 256, 256), 256), None)
        return carry

    lax.fori_loop(1, rows // 256, weigh_more, 0)

    arrived(pf.at[0, a_dn, 0], X_UP0)
    send(pf.at[0, a_dn, 0], pf.at[0, a_dn, 0], X_UPF, up)
    to_pair(1, a_dn, 0)
    arrived(pf.at[0, a_up, 1], X_DN1)
    send(pf.at[0, a_up, 1], pf.at[0, a_up, 1], X_DNF, dn)
    to_pair(2, a_up, 1)
    arrived(pf.at[0, a_dn, 1], X_UP1)
    to_pair(1, a_dn, 1)
    arrived(pf.at[0, a_up, 0], X_DN0)
    to_pair(2, a_up, 0)

    def gathered(k, carry):
        zk = z_at(-k)
        arrived(wg.at[c, 0, zk], A2A + k - 1)
        send(wg.at[c, 0, zk], wg.at[c, 0, zk], WPA + k, pair)
        yk = y_at(-k)
        arrived(wg.at[c, 1, yk], A2B + k - 1)
        send(wg.at[c, 1, yk], wg.at[c, 1, yk], WPB + k, pair)
        return carry

    lax.fori_loop(1, RING, gathered, 0)

    arrived(pf.at[0, a_far, 0], X_UPF)
    to_pair(3, a_far, 0)
    arrived(pf.at[0, a_far, 1], X_DNF)
    to_pair(3, a_far, 1)

    def from_pair(k, carry):
        arrived(wg.at[1 - c, 0, z_at(-k)], WPA + k)
        arrived(wg.at[1 - c, 1, y_at(-k)], WPB + k)
        return carry

    lax.fori_loop(0, RING, from_pair, 0)

    def natural(zz, carry):
        at = pl.ds(pl.multiple_of(zz * 128, 128), 128)
        for core in range(2):
            wq[2 * core, at] = wg[core, 0, zz].reshape(128, 256)
            wq[2 * core + 1, at] = wg[core, 1, :, zz].reshape(128, 256)
        return carry

    lax.fori_loop(0, RING, natural, 0)
    arrived(gx.at[pl.ds(slots, 16)], G_NEXT)

    def partial_of(index):
        at = pl.ds(pl.multiple_of(index * 256, 256), 256)
        value = dot_nt(gx[:, 0:256], wq[0, at])
        for q in range(1, 4):
            value = value + dot_nt(gx[:, 256 * q:256 * q + 256], wq[q, at])
        return value.astype(BF16)

    part[0] = partial_of(a_far)
    send(part.at[0, pl.ds(0, half)], cr_up, C_UPR, up)
    send(part.at[0, pl.ds(half, half + 16)], cr_dn, C_DNR, dn)
    part[1] = partial_of(a_up)
    send(part.at[1, pl.ds(half, half + 16)], c_up.at[pl.ds(half, half + 16)], C_UPD, up)
    part[2] = partial_of(a_dn)
    send(part.at[2, pl.ds(0, half)], c_dn.at[pl.ds(0, half)], C_DND, dn)
    part[3] = partial_of(a)

    for step, index in ((0, a), (1, a_dn), (2, a_up), (3, a_far)):
        for part_half in range(2):
            arrived(pf.at[1, index, part_half], PF_PAIR + 2 * step + part_half)
    copy_gc.wait()
    arrived(gc.at[1], G_PAIR)

    def grad_block(i, carry):
        value = None
        for core in range(2):
            for part_half in range(2):
                term = dot_tn(
                    pf[core, i, part_half], gc[core, half * part_half:half * part_half + half, :]
                )
                value = term if value is None else value + term
        value = value.astype(BF16)
        for zz in range(2):
            for yy in range(RING):
                at = (zz * RING + yy) * 16
                sa[yy, 2 * i + zz] = value[at:at + 16, 0:256]
                sb[2 * i + zz, yy] = value[at:at + 16, 256:512]
        return carry

    lax.fori_loop(0, 4, grad_block, 0)

    def reduce_send(k, carry):
        send(sa.at[y_at(k)], ra.at[k - 1], D1A + k - 1, dev_y(k))
        send(sb.at[z_at(k)], rb.at[k - 1], D1B + k - 1, dev_z(k))
        return carry

    lax.fori_loop(1, RING, reduce_send, 0)

    arrived(cr_up, C_UPR)
    cs_up[...] = (cr_up[...].astype(F32) + part[1, 0:half].astype(F32)).astype(BF16)
    send(cs_up, c_up.at[pl.ds(0, half)], C_UPS, up)
    arrived(cr_dn, C_DNR)
    cs_dn[...] = (cr_dn[...].astype(F32) + part[2, half:half + half + 16].astype(F32)).astype(BF16)
    send(cs_dn, c_dn.at[pl.ds(half, half + 16)], C_DNS, dn)

    def latent(q, carry):
        for part_half in range(2):
            value = dot(pf[0, 0, part_half], wq[q, 0:256])
            for index in range(1, 4):
                value = value + dot(
                    pf[0, index, part_half], wq[q, 256 * index:256 * index + 256]
                )
            lat[q, half * part_half:half * part_half + half] = value.astype(BF16)
        return carry

    lax.fori_loop(0, 4, latent, 0)
    copies = []
    for q in range(4):
        copies.append(
            pltpu.make_async_copy(lat.at[q], lat_hbm.at[:, pl.ds(256 * q, 256)], loc.at[3 + q])
        )
        copies[-1].start()

    def reduced(k, carry):
        arrived(ra.at[k - 1], D1A + k - 1)
        arrived(rb.at[k - 1], D1B + k - 1)
        return carry

    lax.fori_loop(1, RING, reduced, 0)
    sum_a, sum_b = sa[y].astype(F32), sb[z].astype(F32)
    for k in range(RING - 1):
        sum_a = sum_a + ra[k].astype(F32)
        sum_b = sum_b + rb[k].astype(F32)
    ta[...] = sum_a.astype(BF16)
    tb[...] = sum_b.astype(BF16)

    def reduce_more(k, carry):
        send(ta.at[z_at(k)], ua.at[k - 1], D2A + k - 1, dev_z(k))
        send(tb.at[y_at(k)], ub.at[k - 1], D2B + k - 1, dev_y(k))
        return carry

    lax.fori_loop(1, RING, reduce_more, 0)

    arrived(c_up.at[pl.ds(half, half + 16)], C_UPD)
    arrived(c_dn.at[pl.ds(0, half)], C_DND)
    arrived(c_up.at[pl.ds(0, half)], C_UPS)
    arrived(c_dn.at[pl.ds(half, half + 16)], C_DNS)
    grad = part[3].astype(F32) + c_up[...].astype(F32) + c_dn[...].astype(F32)
    zv[:, 0:256], zv[:, 256:512] = split(grad[:slots])
    prev_grad = grad[slots:slots + 1]

    def byte_grad(at, extra):
        got = dot(hot_t[at], zv[...])
        grad_rows = got[:, 0:256] + got[:, 256:512]
        if extra is not None:
            grad_rows = grad_rows + extra
        high, low = split(grad_rows * diff_s[at])
        inner = dot(high, head_ones) + dot(low, head_ones)
        gb[at] = (share_s[at] * grad_rows + coef_s[at] * inner).astype(BF16)

    byte_grad(pl.ds(0, 256), lead_rows(lead8 * prev_grad, 256))

    def byte_more(i, carry):
        byte_grad(pl.ds(pl.multiple_of(i * 256, 256), 256), None)
        return carry

    lax.fori_loop(1, rows // 256, byte_more, 0)
    copies.append(pltpu.make_async_copy(gb, gb_hbm, loc.at[7]))
    copies[-1].start()

    def reduced_more(k, carry):
        arrived(ua.at[k - 1], D2A + k - 1)
        arrived(ub.at[k - 1], D2B + k - 1)
        return carry

    lax.fori_loop(1, RING, reduced_more, 0)
    sum_a, sum_b = ta[z].astype(F32), tb[y].astype(F32)
    for k in range(RING - 1):
        sum_a = sum_a + ua[k].astype(F32)
        sum_b = sum_b + ub[k].astype(F32)
    grad_scale = 1.0 / math.sqrt(n_seq * slots)
    both = jnp.concatenate([sum_a, sum_b], axis=1) * grad_scale
    fin_s[...] = jnp.where(first, both[8:16], both[0:8])
    send(fin_s, fin_r, F_PAIR, pair)
    mine = jnp.where(first, both[0:8], both[8:16])
    arrived(fin_r, F_PAIR)
    other = fin_r[...]
    gw_ref[:, 0:512] = jnp.where(first, mine, other)
    gw_ref[:, 512:1024] = jnp.where(first, other, mine)

    sent(w32, W_PAIR)
    sent(hx.at[pl.ds(0, 16)], H_NEXT)
    sent(hx.at[pl.ds(0, 16)], H_PREV)
    sent(st_p, S_NEXT)
    sent(st_n, S_PREV)
    sent(gl_send, G_NEXT)
    sent(gc.at[0], G_PAIR)
    sent(wg.at[c, 0, z], WPA)
    sent(wg.at[c, 1, y], WPB)

    def all_sent(k, carry):
        sent(wg.at[c, 0, z, y], A1A + k - 1)
        sent(wg.at[c, 1, y, z], A1B + k - 1)
        sent(wg.at[c, 0, z], A2A + k - 1)
        sent(wg.at[c, 1, y], A2B + k - 1)
        sent(wg.at[c, 0, z], WPA + k)
        sent(wg.at[c, 1, y], WPB + k)
        sent(sa.at[y], D1A + k - 1)
        sent(sb.at[z], D1B + k - 1)
        sent(ta.at[z], D2A + k - 1)
        sent(tb.at[y], D2B + k - 1)
        return carry

    lax.fori_loop(1, RING, all_sent, 0)
    for slot in range(X_UP0, X_DNF + 1):
        sent(pf.at[0, a, 0], slot)
    for slot in range(PF_PAIR, PF_PAIR + 8):
        sent(pf.at[0, a, 0], slot)
    sent(part.at[0, pl.ds(0, half)], C_UPR)
    sent(part.at[0, pl.ds(half, half + 16)], C_DNR)
    sent(part.at[1, pl.ds(half, half + 16)], C_UPD)
    sent(part.at[2, pl.ds(0, half)], C_DND)
    sent(cs_up, C_UPS)
    sent(cs_dn, C_DNS)
    sent(fin_s, F_PAIR)
    for copy in copies:
        copy.wait()


def shards(byte_hidden, patch_start, pool_query, in_weight, latent_grad):
    rows, feats = byte_hidden.shape
    slots, width = latent_grad.shape
    half = slots // 2
    any_spec = pl.BlockSpec(memory_space=pl.ANY)
    vmem = pl.BlockSpec(memory_space=pltpu.VMEM)

    def buf(*shape, dtype=BF16):
        return pltpu.VMEM(shape, dtype)

    scratch = [
        buf(rows + 128, feats),
        buf(8, rows, dtype=F32), buf(8, 128, dtype=F32), buf(8, 128, dtype=F32),
        buf(8, width, dtype=F32), buf(8, width, dtype=F32),
        buf(2, 2, RING, RING, 16, 256),
        buf(4, 1024, 256),
        buf(slots + 16, width), buf(16, width), buf(2, slots, 512),
        buf(slots + 16, rows + 128), buf(rows, slots),
        buf(rows + 128, 1024), buf(rows + 128, feats, dtype=F32), buf(rows + 128, feats, dtype=F32),
        buf(8, 128, dtype=F32), buf(8, 128, dtype=F32),
        buf(slots, 1024),
        buf(rows, feats, dtype=F32), buf(rows, feats, dtype=F32), buf(rows, feats, dtype=F32),
        buf(2, 4, 2, half, 256),
        buf(4, slots + 16, 256),
        buf(half, 256), buf(half + 16, 256), buf(half, 256), buf(half + 16, 256),
        buf(slots + 16, 256), buf(slots + 16, 256),
        buf(slots, 512),
        buf(4, slots, 256), buf(rows, feats),
        buf(RING, RING, 16, 256), buf(RING, RING, 16, 256),
        buf(RING - 1, RING, 16, 256), buf(RING - 1, RING, 16, 256),
        buf(RING, 16, 256), buf(RING, 16, 256),
        buf(RING - 1, 16, 256), buf(RING - 1, 16, 256),
        buf(8, 512, dtype=F32), buf(8, 512, dtype=F32),
        pltpu.SemaphoreType.DMA((8,)),
        pltpu.SemaphoreType.DMA((SLOTS_SEM,)),
        pltpu.SemaphoreType.DMA((SLOTS_SEM,)),
    ]
    return pl.pallas_call(
        kernel,
        out_shape=(
            jax.ShapeDtypeStruct((slots, width), BF16),
            jax.ShapeDtypeStruct((8, width), F32),
            jax.ShapeDtypeStruct((rows, feats), BF16),
        ),
        in_specs=[any_spec, vmem, vmem, vmem, any_spec],
        out_specs=(any_spec, vmem, any_spec),
        scratch_shapes=scratch,
        compiler_params=pltpu.CompilerParams(
            collective_id=0, has_side_effects=True, vmem_limit_bytes=48 * 1024 * 1024
        ),
        name="patch_pool",
    )(
        byte_hidden, patch_start.reshape(1, rows), pool_query.reshape(1, feats),
        in_weight, latent_grad,
    )


def solution(mesh):
    in_specs = (P("seq", "mp"), P("seq"), P("mp"), P("seq", "mp"), P("seq", "mp"))
    out_specs = (P("seq", "mp"), P("seq", "mp"), P("seq", "mp"))
    return jax.shard_map(shards, mesh=mesh, in_specs=in_specs, out_specs=out_specs, check_vma=False)
```

time: 374 us -> 72.9 us (0.19); the launches traced: 369 us -> 72.6 us
  waiting for transfers between devices: 266 us -> 0 us
  Pallas kernels: 0 us -> 65.3 us
  other arithmetic: 31.8 us -> 0 us
  starting transfers between devices: 25.2 us -> 0 us
  local copies, waits for them, and re-layouts: 21.8 us -> 6.7 us
  between operations: 14.7 us -> 0.65 us
  matrix products: 9.55 us -> 0 us
    reduce_scatter x1 -> x0, waiting for transfers between devices: 165 us -> none  [shards(): lax.psum_scatter(lax.dot_general(pooled_full, latent_grad, (((0,), (0,)),...]
    all_gather x2 -> x0, waiting for transfers between devices: 100 us -> none  [the longest x1 72.4 us: shards(): weight_full = lax.all_gather(in_weight, 'seq', axis=0, tiled=True)]
    pallas_call x0 -> x1, Pallas kernels: none -> 65.3 us  [shards(): pl.pallas_call(kernel, out_shape=(jax.ShapeDtypeStruct((slots, width), BF...]
    ppermute x5 -> x0, starting transfers between devices: 20.8 us -> none  [from_behind(): lax.ppermute(value, axis, [(source, source + steps) for source in range(l...]
    scatter-add x2 -> x0, other arithmetic: 16 us -> none  [the longest x1 9.13 us: shards(): numer = jax.ops.segment_sum(weighted * keep_own, inside, num_segments=slots)]
    gather x4 -> x0, local copies, waits for them, and re-layouts: 11.2 us -> none  [the longest x1 4.68 us: shards(): jnp.take(pooled, inside, axis=0)]
    dot_general x3 -> x0, matrix products: 9.55 us -> none  [the longest x1 4.44 us: shards(): lax.dot_general(pooled_full, latent_grad, (((0,), (0,)), ((), ())), prefe...]
    unnamed x12 -> x13, local copies, waits for them, and re-layouts: 0.04 us -> 6.7 us
  transfers between devices with their start and end apart: 9 -> 0, of which waited for: 3 -> 0; matrix products, arithmetic and copies ran while one was open for 14% -> 0% of each run, Pallas kernels for 0% -> 0%
where the time goes in v1:
time: 72.9 us; the launch traced here: 72.6 us
  Pallas kernels  65.3 us (90%)
  local copies, waits for them, and re-layouts  6.7 us (9%)
    pallas_call x1, Pallas kernels, shards(): pl.pallas_call(kernel, out_shape=(jax.ShapeDtypeStruct((slots, width), BF...  65.3 us
    unnamed x13, local copies, waits for them, and re-layouts  6.7 us

profile of v1, /device:TPU:1, one launch (start us, length us, event | category | flops | bytes accessed | tf_op | source)
XLA Modules:
  0.0 72.6 jit_solution(6234382411991694374)
XLA Ops:
  0.6 0.0 copy-start.4
  0.6 0.6 copy-done.4
  1.3 0.0 copy-start
  1.3 1.2 %copy-done = bf16[512,1024]{1,0:T(8,128)(2,1)S(1)} copy-done((bf16[512,1024]{1,0:T(8,128)(2,1)S(1)}, bf16[512,1024]{1,0:T(8,128)(2,1)}, u32[]{:S(2)}) %copy-start) | copy-done | bytes 1048600
  2.5 0.0 copy-start.1
  2.5 1.0 %copy-done.1 = bf16[1024,256]{1,0:T(8,128)(2,1)S(1)} copy-done((bf16[1024,256]{1,0:T(8,128)(2,1)S(1)}, bf16[1024,256]{1,0:T(8,128)(2,1)}, u32[]{:S(2)}) %copy-start.1) | copy-done | bytes 524312
  3.6 0.0 copy-start.2
  3.6 0.7 copy-done.2
  4.3 0.0 copy-start.3
  4.3 0.7 copy-done.3
  5.0 65.3 %patch_pool.1 = (bf16[512,1024]{1,0:T(8,128)(2,1)S(1)}, f32[8,1024]{1,0:T(8,128)S(1)}, bf16[1024,256]{1,0:T(8,128)(2,1)S(1)}) custom-call(bf16[1024,256]{1,0:T(8,128)(2,1)S(1)} %copy-done.1, s32[1,1024]{1,0:T(1,128)S(1)} %bitcast.1, bf16[1,256]{1,0:T(2,128)(2,1)S(1)} %reshape.13.q_ref, bf16[8,1024]{1,0:T(8,128)(2,1)S(1)} %copy-done.2, ...), custom_call_target="tpu_custom_call" | custom-call | tf_op jit(solution)/shard_map/patch_pool/pallas_call | solution.py:553
  70.2 1.0 %copy.11 = bf16[512,1024]{1,0:T(8,128)(2,1)} copy(bf16[512,1024]{1,0:T(8,128)(2,1)S(1)} %get-tuple-element.6) | data formatting | bytes 2097152
  71.2 0.6 copy.12
  71.8 0.8 %copy.13 = bf16[1024,256]{1,0:T(8,128)(2,1)} copy(bf16[1024,256]{1,0:T(8,128)(2,1)S(1)} %get-tuple-element.8) | data formatting | bytes 1048576
  (1 shorter events, 0.0 us)
Async XLA Ops:
  0.6 0.7 copy-start.4
  1.3 1.2 %copy-start = (bf16[512,1024]{1,0:T(8,128)(2,1)S(1)}, bf16[512,1024]{1,0:T(8,128)(2,1)}, u32[]{:S(2)}) copy-start(bf16[512,1024]{1,0:T(8,128)(2,1)} %g_hbm.1) | copy-start | bytes 3145732
  2.5 1.0 %copy-start.1 = (bf16[1024,256]{1,0:T(8,128)(2,1)S(1)}, bf16[1024,256]{1,0:T(8,128)(2,1)}, u32[]{:S(2)}) copy-start(bf16[1024,256]{1,0:T(8,128)(2,1)} %h_hbm.1) | copy-start | bytes 1572868
  3.6 0.7 copy-start.2
  4.3 0.7 copy-start.3

commit v2 on v1

v2 whole, which is shorter than its diff:
```python
import math

import jax
import jax.numpy as jnp
from jax import lax
from jax.experimental import pallas as pl
from jax.experimental.pallas import tpu as pltpu
from jax.sharding import PartitionSpec as P

HEAD_DIM = 64
SOFT_CAP = 20.0
RING = 8
F32 = jnp.float32
BF16 = jnp.bfloat16
MESH = pl.DeviceIdType.MESH
VMEM_LIMIT = 60 * 1024 * 1024

W_PAIR, H_NEXT, H_PREV, S_NEXT, S_PREV, G_NEXT, G_PAIR, F_PAIR = range(8)
X_UP0, X_UP1, X_UPF, X_DN1, X_DN0, X_DNF = range(8, 14)
C_UPR, C_UPD, C_UPS, C_DNR, C_DND, C_DNS = range(14, 20)
PF_PAIR = 20
A1A, A1B, A2A, A2B = 28, 36, 44, 52
WPA, WPB = 60, 68
D1A = 76
D1B, D2A, D2B = 108, 116, 124
SLOTS_SEM = 132


def dot(a, b):
    return jnp.dot(a, b, preferred_element_type=F32)


def dot_nt(a, b):
    return lax.dot_general(a, b, (((1,), (1,)), ((), ())), preferred_element_type=F32)


def dot_tn(a, b):
    return lax.dot_general(a, b, (((0,), (0,)), ((), ())), preferred_element_type=F32)


def split(value):
    high = value.astype(BF16)
    return high, (value - high.astype(F32)).astype(BF16)


def iota(shape, dim):
    return lax.broadcasted_iota(jnp.int32, shape, dim)


def kernel(
    h_hbm, st_hbm, q_hbm, w_hbm, g_hbm,
    lat_hbm, gw_hbm, gb_hbm,
    lat_ref, gw_ref, gb_ref, hx, st_own, q_own, st8, st_n, st_p, w_own, w32, w32r, wg, wq, gx, gl_send, gc,
    hot, hot_t, xs, ws, ts, yv, share_s, diff_s, coef_s,
    pf, part, cr_up, cr_dn, cs_up, cs_dn, c_up, c_dn, zv,
    sa, sb, ra, rb, ta, tb, ua, ub, fin_s, fin_r,
    loc, ss, rs,
):
    s = lax.axis_index("seq")
    a = lax.axis_index("mp")
    n_seq, n_mp = lax.axis_size("seq"), lax.axis_size("mp")
    slots = g_hbm.shape[0]
    rows, feats = h_hbm.shape
    half = slots // 2
    c = lax.rem(s, 2)
    y = lax.rem(lax.div(s, 2), RING)
    z = lax.div(s, 2 * RING)
    first = c == 0

    def wrap(value, size):
        return lax.rem(value + size, size)

    pair = (s + 1 - 2 * c, a)
    nxt = (wrap(s + 1, n_seq), a)
    prv = (wrap(s - 1, n_seq), a)
    a_up, a_dn, a_far = wrap(a + 1, n_mp), wrap(a - 1, n_mp), wrap(a + 2, n_mp)
    up, dn = (s, a_up), (s, a_dn)

    def y_at(k):
        return wrap(y + k, RING)

    def z_at(k):
        return wrap(z + k, RING)

    def dev_y(k):
        return ((z * RING + y_at(k)) * 2 + c, a)

    def dev_z(k):
        return ((z_at(k) * RING + y) * 2 + c, a)

    def remote(src, dst, slot, device):
        return pltpu.make_async_remote_copy(
            src_ref=src, dst_ref=dst, send_sem=ss.at[slot], recv_sem=rs.at[slot],
            device_id=device, device_id_type=MESH,
        )

    flying, landing = {}, {}

    def note(slot, ref):
        flying[slot] = ref
        landing[slot] = ref

    def send(src, dst, slot, device):
        remote(src, dst, slot, device).start()
        if isinstance(slot, int):
            note(slot, src)

    def arrived(dst, slot):
        remote(dst, dst, slot, pair).wait_recv()
        if isinstance(slot, int):
            landing.pop(slot)

    def ring(body, low=1, high=RING):
        def step(k, carry):
            body(k)
            return carry

        lax.fori_loop(low, high, step, 0)

    def noted(base, ref, low=1, high=RING):
        for k in range(low, high):
            note(base + k, ref)

    def landed(base, low=1, high=RING):
        for k in range(low, high):
            landing.pop(base + k)

    copies = []

    def fetch(src, dst):
        copy = pltpu.make_async_copy(src, dst, loc.at[len(copies)])
        copy.start()
        copies.append(copy)
        return len(copies) - 1

    def fetched(index):
        copies[index].wait()
        copies[index] = None

    def drain():
        for copy in copies:
            if copy is not None:
                copy.wait()
        for slot, ref in landing.items():
            remote(ref, ref, slot, pair).wait_recv()
        for slot, ref in flying.items():
            remote(ref, ref, slot, pair).wait_send()

    barrier = pltpu.get_barrier_semaphore()

    def greet(device):
        pl.semaphore_signal(barrier, inc=1, device_id=device, device_id_type=MESH)

    for device in (pair, nxt, prv, up, dn):
        greet(device)

    def greet_ring(k):
        greet(dev_y(k))
        greet(dev_z(k))

    ring(greet_ring)

    own_cols = pl.ds(pl.multiple_of(c * 512, 512), 512)
    pair_cols = pl.ds(pl.multiple_of((1 - c) * 512, 512), 512)
    copy_w = fetch(w_hbm, w_own)
    copy_st = fetch(st_hbm, st_own)
    copy_q = fetch(q_hbm, q_own)
    copy_h = fetch(h_hbm, hx.at[pl.ds(0, rows)])
    copy_g = fetch(g_hbm, gx.at[pl.ds(0, slots)])
    copy_gc = fetch(g_hbm.at[:, own_cols], gc.at[0])
    hx[rows + 16:rows + 112, :] = jnp.zeros((96, feats), BF16)
    same = lax.div(iota((feats, feats), 0), HEAD_DIM) == lax.div(iota((feats, feats), 1), HEAD_DIM)
    fetched(copy_q)
    query = q_own[...].astype(F32)
    query = jnp.concatenate([query[0:1], query[1:2]], axis=1)
    q_mat = jnp.where(same, jnp.broadcast_to(query, (feats, feats)), 0.0).astype(BF16)
    head_ones = jnp.where(same, 1.0, 0.0).astype(BF16)
    inv_root = 1.0 / math.sqrt(HEAD_DIM)
    fetched(copy_w)
    w32[...] = w_own[...].astype(F32)
    fetched(copy_st)
    st8[...] = jnp.broadcast_to(st_own[...].astype(F32), st8.shape)

    pl.semaphore_wait(barrier, 5 + 2 * (RING - 1))

    send(w32, w32r, W_PAIR, pair)
    send(h_hbm.at[pl.ds(rows - 16, 16)], hx.at[pl.ds(rows + 112, 16)], H_NEXT, nxt)
    send(h_hbm.at[pl.ds(0, 16)], hx.at[pl.ds(rows, 16)], H_PREV, prv)
    send(st8.at[:, pl.ds(rows - 128, 128)], st_p, S_NEXT, nxt)
    send(st8.at[:, pl.ds(0, 128)], st_n, S_PREV, prv)

    arrived(w32r, W_PAIR)
    w_mine, w_other = w32[...], w32r[...]
    w16 = jnp.concatenate(
        [jnp.where(first, w_mine, w_other), jnp.where(first, w_other, w_mine)], axis=0
    )
    w_half = jnp.where(first, w16[:, :512], w16[:, 512:]).astype(BF16)
    wg[c, 0, z, y] = w_half[:, :256]
    wg[c, 1, y, z] = w_half[:, 256:]

    def lines(k):
        send(wg.at[c, 0, z, y], wg.at[c, 0, z, y], A1A + k, dev_y(k))
        send(wg.at[c, 1, y, z], wg.at[c, 1, y, z], A1B + k, dev_z(k))

    ring(lines)
    noted(A1A, wg.at[c, 0, z, y])
    noted(A1B, wg.at[c, 1, y, z])
    send(g_hbm.at[:, pair_cols], gc.at[1], G_PAIR, pair)

    def score(start, size):
        at = pl.ds(start, size)
        h = hx[at]
        t = jnp.tanh(dot_nt(h, q_mat) * (inv_root / SOFT_CAP))
        w = jnp.exp(SOFT_CAP * t)
        ws[at] = w
        ts[at] = t
        xs[at, 0:256], xs[at, 256:512] = split(w * h.astype(F32))
        xs[at, 512:768], xs[at, 768:1024] = split(w)

    fetched(copy_h)

    def score_own(i):
        score(pl.multiple_of(i * 256, 256), 256)

    ring(score_own, 0, rows // 256)

    r128, c128 = iota((128, 128), 0), iota((128, 128), 1)
    upper = jnp.where(r128 <= c128, 1.0, 0.0).astype(BF16)
    lower = jnp.where(c128 <= r128, 1.0, 0.0).astype(BF16)
    ones = jnp.ones((128, 128), BF16)
    hot_rows = hot.shape[0]
    slot_col = iota((hot_rows, 128), 0).astype(F32)
    lane = iota((128, 128), 1).astype(F32)
    total = jnp.zeros((8, 128), F32)
    lead8 = None
    for k in range(rows // 128):
        st_k = st8[:, 128 * k:128 * k + 128].astype(BF16)
        row_id = total + dot(st_k, upper) - 1.0
        row_id = jnp.where(row_id < 0.0, F32(slots), row_id)
        hot[:, 128 * k:128 * k + 128] = jnp.where(slot_col == row_id[0:1], 1.0, 0.0).astype(BF16)
        st_t = jnp.broadcast_to(st8[0:1, 128 * k:128 * k + 128], (128, 128)).astype(BF16)
        col_id = dot_nt(lower, st_t) + total[0:1] - 1.0
        if k == 0:
            lead8 = jnp.where(col_id[0:8] < 0.0, 1.0, 0.0).astype(F32)
        for j in range(slots // 128):
            hot_t[128 * k:128 * k + 128, 128 * j:128 * j + 128] = jnp.where(
                col_id == lane + 128.0 * j, 1.0, 0.0
            ).astype(BF16)
        total = total + dot(st_k, ones)
    lead8 = jnp.concatenate([lead8, lead8], axis=1)

    def planes(k):
        arrived(wg.at[c, 0, z, y], A1A + k)
        arrived(wg.at[c, 1, y, z], A1B + k)

    ring(planes)
    landed(A1A)
    landed(A1B)
    mine_a, mine_b = wg.at[c, 0, z], wg.at[c, 1, y]
    for k in (2, 6, 1, 7):
        send(mine_a, mine_a, A2A + k, dev_z(k))
        send(mine_b, mine_b, A2B + k, dev_y(k))
    send(mine_a, mine_a, WPA, pair)
    send(mine_b, mine_b, WPB, pair)

    arrived(hx.at[pl.ds(rows + 112, 16)], H_NEXT)
    arrived(hx.at[pl.ds(rows, 16)], H_PREV)
    arrived(st_p, S_NEXT)
    arrived(st_n, S_PREV)
    score(rows, 128)
    after = jnp.where((r128 <= c128) & (c128 < 64), 1.0, 0.0).astype(BF16)
    before = jnp.where((r128 > c128) & (c128 >= 64), 1.0, 0.0).astype(BF16)
    starts_n = jnp.where(s == n_seq - 1, 1.0, st_n[...]).astype(BF16)
    starts_p = jnp.where(s == 0, 1.0, st_p[...]).astype(BF16)
    count = dot(starts_n, after) + dot(starts_p, before)
    halo_slot = jnp.where(iota((8, 128), 1) < 64, total - 1.0, F32(slots))
    halo_slot = jnp.where(count == 0.0, halo_slot, -9.0)
    hot[:, rows:rows + 128] = jnp.where(slot_col == halo_slot[0:1], 1.0, 0.0).astype(BF16)

    onehot = hot[...]
    denom = dot(onehot, xs[:, 512:768]) + dot(onehot, xs[:, 768:1024])
    numer = dot(onehot, xs[:, 0:256]) + dot(onehot, xs[:, 256:512])
    live = denom > 0.0
    denom = jnp.where(live, denom, 1.0)
    pooled = jnp.where(live, numer / denom, 0.0)
    pf[0, a, 0] = pooled[:half].astype(BF16)
    pf[0, a, 1] = pooled[half:slots].astype(BF16)
    send(pf.at[0, a, 0], pf.at[0, a, 0], X_UP0, up)
    send(pf.at[0, a, 1], pf.at[0, a, 1], X_DN1, dn)
    send(pf.at[0, a, 1], pf.at[0, a, 1], X_UP1, up)
    send(pf.at[0, a, 0], pf.at[0, a, 0], X_DN0, dn)

    def to_pair(step, index, part_half):
        send(pf.at[0, index, part_half], pf.at[1, index, part_half],
             PF_PAIR + 2 * step + part_half, pair)

    to_pair(0, a, 0)
    to_pair(0, a, 1)

    fetched(copy_g)
    pick = iota((16, slots), 1).astype(F32) == (total[0:1, 0:1] - 1.0)
    pick = jnp.where(pick & (iota((16, slots), 0) == 0), 1.0, 0.0).astype(BF16)
    gl_send[...] = dot(pick, gx[0:slots, :]).astype(BF16)
    send(gl_send, gx.at[pl.ds(slots, 16)], G_NEXT, nxt)

    yv[:, 0:256], yv[:, 256:512] = split(pooled[:slots])
    yv[:, 512:768], yv[:, 768:1024] = split(denom[:slots])
    prev_pool, prev_den = pooled[slots:slots + 1], denom[slots:slots + 1]

    def lead_rows(value8, size):
        return jnp.concatenate([value8, jnp.zeros((size - 8, feats), F32)], axis=0)

    def weigh(at, extra):
        got = dot(hot_t[at], yv[...])
        pool_rows = got[:, 0:256] + got[:, 256:512]
        den_rows = got[:, 512:768] + got[:, 768:1024]
        if extra is not None:
            pool_rows = pool_rows + extra[0]
            den_rows = den_rows + extra[1]
        t = ts[at]
        share = ws[at] / den_rows
        share_s[at] = share
        diff_s[at] = hx[at].astype(F32) - pool_rows
        coef_s[at] = share * (1.0 - t * t) * (query * inv_root)

    weigh(pl.ds(0, 256), (lead_rows(lead8 * prev_pool, 256), lead_rows(lead8 * prev_den, 256)))

    def weigh_more(i):
        weigh(pl.ds(pl.multiple_of(i * 256, 256), 256), None)

    ring(weigh_more, 1, rows // 256)

    def whole(kind, k):
        return wg.at[c, kind, z_at(-k) if kind == 0 else y_at(-k)]

    def piece(kind, k, lower_half):
        return wg.at[c, kind, z_at(-k) if kind == 0 else y_at(-k), pl.ds(0 if lower_half else 4, 4)]

    kinds = ((0, A2A, dev_z, WPA), (1, A2B, dev_y, WPB))
    for kind, base, dev, _ in kinds:
        arrived(whole(kind, 2), base + 2)
        send(whole(kind, 2), whole(kind, 2), base + 3, dev(1))
        send(piece(kind, 2, True), piece(kind, 2, True), base + 4, dev(2))
        arrived(whole(kind, 6), base + 6)
        send(whole(kind, 6), whole(kind, 6), base + 5, dev(-1))
        send(piece(kind, 6, False), piece(kind, 6, False), base, dev(-2))

    arrived(pf.at[0, a_dn, 0], X_UP0)
    send(pf.at[0, a_dn, 0], pf.at[0, a_dn, 0], X_UPF, up)
    arrived(pf.at[0, a_up, 1], X_DN1)
    send(pf.at[0, a_up, 1], pf.at[0, a_up, 1], X_DNF, dn)
    to_pair(1, a_dn, 0)
    to_pair(2, a_up, 1)
    for kind, base, dev, pair_base in kinds:
        for k in (2, 6, 1, 7):
            if k in (1, 7):
                arrived(whole(kind, k), base + k)
            send(whole(kind, k), whole(kind, k), pair_base + k, pair)
    arrived(pf.at[0, a_dn, 1], X_UP1)
    to_pair(1, a_dn, 1)
    arrived(pf.at[0, a_up, 0], X_DN0)
    to_pair(2, a_up, 0)
    for kind, base, dev, pair_base in kinds:
        for k in (3, 5, 4):
            if k == 4:
                arrived(piece(kind, k, True), base + 4)
                arrived(piece(kind, k, False), base)
            else:
                arrived(whole(kind, k), base + k)
            send(whole(kind, k), whole(kind, k), pair_base + k, pair)
    arrived(pf.at[0, a_far, 0], X_UPF)
    to_pair(3, a_far, 0)
    arrived(pf.at[0, a_far, 1], X_DNF)
    to_pair(3, a_far, 1)

    for step, index in ((0, a), (1, a_dn), (2, a_up), (3, a_far)):
        for part_half in range(2):
            arrived(pf.at[1, index, part_half], PF_PAIR + 2 * step + part_half)
    fetched(copy_gc)
    arrived(gc.at[1], G_PAIR)

    def block_at(i):
        turn = jnp.where(i == 0, 2, jnp.where(i == 1, 1, jnp.where(i == 2, 3, 0)))
        return lax.rem(lax.div(z, 2) + turn, 4)

    def grad_block(i):
        index = block_at(i)
        value = None
        for core in range(2):
            for part_half in range(2):
                term = dot_tn(
                    pf[core, index, part_half], gc[core, half * part_half:half * part_half + half, :]
                )
                value = term if value is None else value + term
        value = value.astype(BF16)
        for zz in range(2):
            for yy in range(RING):
                at = (zz * RING + yy) * 16
                sa[yy, 2 * index + zz] = value[at:at + 16, 0:256]
                sb[2 * index + zz, yy] = value[at:at + 16, 256:512]
        two = pl.ds(2 * index, 2)

        def spread(k):
            send(sa.at[y_at(k), two], ra.at[k - 1, two], D1A + 8 * i + k, dev_y(k))

        ring(spread)
        for zz in range(2):
            k = wrap(2 * index + zz - z, RING)

            @pl.when(k > 0)
            def _():
                send(sb.at[2 * index + zz], rb.at[k - 1], D1B + k, dev_z(k))

    ring(grad_block, 0, 4)
    for i in range(4):
        noted(D1A + 8 * i, sa.at[0, pl.ds(0, 2)])
    noted(D1B, sb.at[0])

    def from_pair(k):
        arrived(wg.at[1 - c, 0, z_at(-k)], WPA + k)
        arrived(wg.at[1 - c, 1, y_at(-k)], WPB + k)

    ring(from_pair, 0)
    landed(WPA, 0)
    landed(WPB, 0)

    def natural(zz):
        at = pl.ds(pl.multiple_of(zz * 128, 128), 128)
        for core in range(2):
            wq[2 * core, at] = wg[core, 0, zz].reshape(128, 256)
            wq[2 * core + 1, at] = wg[core, 1, :, zz].reshape(128, 256)

    ring(natural, 0)
    arrived(gx.at[pl.ds(slots, 16)], G_NEXT)

    def partial_of(index):
        at = pl.ds(pl.multiple_of(index * 256, 256), 256)
        value = dot_nt(gx[:, 0:256], wq[0, at])
        for q in range(1, 4):
            value = value + dot_nt(gx[:, 256 * q:256 * q + 256], wq[q, at])
        return value.astype(BF16)

    upper_rows = pl.ds(half, half + 16)
    lower_rows = pl.ds(0, half)
    part[0] = partial_of(a_far)
    send(part.at[0, lower_rows], cr_up, C_UPR, up)
    send(part.at[0, upper_rows], cr_dn, C_DNR, dn)
    part[1] = partial_of(a_up)
    send(part.at[1, upper_rows], c_up.at[upper_rows], C_UPD, up)
    part[2] = partial_of(a_dn)
    send(part.at[2, lower_rows], c_dn.at[lower_rows], C_DND, dn)

    arrived(cr_up, C_UPR)
    cs_up[...] = (cr_up[...].astype(F32) + part[1, 0:half].astype(F32)).astype(BF16)
    send(cs_up, c_up.at[lower_rows], C_UPS, up)
    arrived(cr_dn, C_DNR)
    cs_dn[...] = (cr_dn[...].astype(F32) + part[2, half:half + half + 16].astype(F32)).astype(BF16)
    send(cs_dn, c_dn.at[upper_rows], C_DNS, dn)
    part[3] = partial_of(a)

    def latent(part_half):
        at = pl.ds(pl.multiple_of(part_half * half, half), half)
        for q in range(4):
            value = dot(pf[0, 0, part_half], wq[q, 0:256])
            for index in range(1, 4):
                value = value + dot(
                    pf[0, index, part_half], wq[q, 256 * index:256 * index + 256]
                )
            lat_ref[at, 256 * q:256 * q + 256] = value.astype(BF16)

    ring(latent, 0, 2)
    fetch(lat_ref, lat_hbm)

    def reduced(k):
        def blocks(i):
            two = pl.ds(2 * block_at(i), 2)
            arrived(ra.at[k - 1, two], D1A + 8 * i + k)

        ring(blocks, 0, 4)
        arrived(rb.at[k - 1], D1B + k)

    ring(reduced)
    for i in range(4):
        landed(D1A + 8 * i)
    landed(D1B)
    sum_a, sum_b = sa[y].astype(F32), sb[z].astype(F32)
    for k in range(RING - 1):
        sum_a = sum_a + ra[k].astype(F32)
        sum_b = sum_b + rb[k].astype(F32)
    ta[...] = sum_a.astype(BF16)
    tb[...] = sum_b.astype(BF16)

    def reduce_more(k):
        send(ta.at[z_at(k)], ua.at[k - 1], D2A + k, dev_z(k))
        send(tb.at[y_at(k)], ub.at[k - 1], D2B + k, dev_y(k))

    ring(reduce_more)
    noted(D2A, ta.at[0])
    noted(D2B, tb.at[0])

    arrived(c_up.at[upper_rows], C_UPD)
    arrived(c_dn.at[lower_rows], C_DND)
    arrived(c_up.at[lower_rows], C_UPS)
    arrived(c_dn.at[upper_rows], C_DNS)
    grad = part[3].astype(F32) + c_up[...].astype(F32) + c_dn[...].astype(F32)
    zv[:, 0:256], zv[:, 256:512] = split(grad[:slots])
    prev_grad = grad[slots:slots + 1]

    def byte_grad(at, extra):
        got = dot(hot_t[at], zv[...])
        grad_rows = got[:, 0:256] + got[:, 256:512]
        if extra is not None:
            grad_rows = grad_rows + extra
        high, low = split(grad_rows * diff_s[at])
        inner = dot(high, head_ones) + dot(low, head_ones)
        gb_ref[at] = (share_s[at] * grad_rows + coef_s[at] * inner).astype(BF16)

    byte_grad(pl.ds(0, 256), lead_rows(lead8 * prev_grad, 256))

    def byte_more(i):
        byte_grad(pl.ds(pl.multiple_of(i * 256, 256), 256), None)

    ring(byte_more, 1, rows // 256)
    fetch(gb_ref, gb_hbm)

    def reduced_more(k):
        arrived(ua.at[k - 1], D2A + k)
        arrived(ub.at[k - 1], D2B + k)

    ring(reduced_more)
    landed(D2A)
    landed(D2B)
    sum_a, sum_b = ta[z].astype(F32), tb[y].astype(F32)
    for k in range(RING - 1):
        sum_a = sum_a + ua[k].astype(F32)
        sum_b = sum_b + ub[k].astype(F32)
    grad_scale = 1.0 / math.sqrt(n_seq * slots)
    both = jnp.concatenate([sum_a, sum_b], axis=1) * grad_scale
    fin_s[...] = jnp.where(first, both[8:16], both[0:8])
    send(fin_s, fin_r, F_PAIR, pair)
    mine = jnp.where(first, both[0:8], both[8:16])
    arrived(fin_r, F_PAIR)
    other = fin_r[...]
    gw_ref[:, 0:512] = jnp.where(first, mine, other)
    gw_ref[:, 512:1024] = jnp.where(first, other, mine)
    fetch(gw_ref, gw_hbm)

    drain()


def place(lat_in, gw_in, gb_in, lat_out, gw_out, gb_out, lat, gw, gb, sem_in, sem_out):
    parts = [(lat_in, lat, lat_out, 256 * i, 256) for i in range(lat.shape[0] // 256)]
    parts += [(gb_in, gb, gb_out, 512 * i, 512) for i in range(gb.shape[0] // 512)]
    parts.append((gw_in, gw, gw_out, 0, 8))
    reads, writes = [], []
    for i, (src, mid, dst, start, size) in enumerate(parts):
        at = pl.ds(start, size)
        reads.append(pltpu.make_async_copy(src.at[at], mid.at[at], sem_in.at[i]))
        writes.append(pltpu.make_async_copy(mid.at[at], dst.at[at], sem_out.at[i]))
    for copy in reads:
        copy.start()
    for read, write in zip(reads, writes):
        read.wait()
        write.start()
    for copy in writes:
        copy.wait()


def shards(byte_hidden, patch_start, pool_query, in_weight, latent_grad):
    rows, feats = byte_hidden.shape
    slots, width = latent_grad.shape
    half = slots // 2
    hbm = pl.BlockSpec(memory_space=pltpu.HBM)

    def buf(*shape, dtype=BF16):
        return pltpu.VMEM(shape, dtype)

    scratch = [
        buf(slots, width), buf(8, width, dtype=F32), buf(rows, feats),
        buf(rows + 128, feats), buf(1, rows, dtype=jnp.int32), buf(2, 128),
        buf(8, rows, dtype=F32), buf(8, 128, dtype=F32), buf(8, 128, dtype=F32),
        buf(8, width), buf(8, width, dtype=F32), buf(8, width, dtype=F32),
        buf(2, 2, RING, RING, 16, 256), buf(4, 1024, 256),
        buf(slots + 16, width), buf(16, width), buf(2, slots, 512),
        buf(slots + 16, rows + 128), buf(rows, slots),
        buf(rows + 128, 1024), buf(rows + 128, feats, dtype=F32), buf(rows + 128, feats, dtype=F32),
        buf(slots, 1024),
        buf(rows, feats, dtype=F32), buf(rows, feats, dtype=F32), buf(rows, feats, dtype=F32),
        buf(2, 4, 2, half, 256), buf(4, slots + 16, 256),
        buf(half, 256), buf(half + 16, 256), buf(half, 256), buf(half + 16, 256),
        buf(slots + 16, 256), buf(slots + 16, 256), buf(slots, 512),
        buf(RING, RING, 16, 256), buf(RING, RING, 16, 256),
        buf(RING - 1, RING, 16, 256), buf(RING - 1, RING, 16, 256),
        buf(RING, 16, 256), buf(RING, 16, 256),
        buf(RING - 1, 16, 256), buf(RING - 1, 16, 256),
        buf(8, 512, dtype=F32), buf(8, 512, dtype=F32),
        pltpu.SemaphoreType.DMA((9,)),
        pltpu.SemaphoreType.DMA((SLOTS_SEM,)),
        pltpu.SemaphoreType.DMA((SLOTS_SEM,)),
    ]
    shapes = (
        jax.ShapeDtypeStruct((slots, width), BF16),
        jax.ShapeDtypeStruct((8, width), F32),
        jax.ShapeDtypeStruct((rows, feats), BF16),
    )
    outs = pl.pallas_call(
        kernel,
        out_shape=shapes,
        in_specs=[hbm] * 5,
        out_specs=(hbm, hbm, hbm),
        scratch_shapes=scratch,
        compiler_params=pltpu.CompilerParams(
            collective_id=0, has_side_effects=True, vmem_limit_bytes=VMEM_LIMIT
        ),
        name="patch_pool",
    )(
        byte_hidden, patch_start.reshape(1, rows), pool_query.reshape(2, feats // 2),
        in_weight, latent_grad,
    )
    return pl.pallas_call(
        place,
        out_shape=shapes,
        in_specs=[hbm] * 3,
        out_specs=(hbm, hbm, hbm),
        scratch_shapes=[
            buf(slots, width), buf(8, width, dtype=F32), buf(rows, feats),
            pltpu.SemaphoreType.DMA((5,)), pltpu.SemaphoreType.DMA((5,)),
        ],
        compiler_params=pltpu.CompilerParams(vmem_limit_bytes=VMEM_LIMIT),
        name="place",
    )(*outs)


def solution(mesh):
    in_specs = (P("seq", "mp"), P("seq"), P("mp"), P("seq", "mp"), P("seq", "mp"))
    out_specs = (P("seq", "mp"), P("seq", "mp"), P("seq", "mp"))
    return jax.shard_map(shards, mesh=mesh, in_specs=in_specs, out_specs=out_specs, check_vma=False)
```

time: 72.9 us -> 63.3 us (0.87)
  local copies, waits for them, and re-layouts: 6.7 us -> 0 us
  Pallas kernels: 65.3 us -> 62.5 us
    unnamed x13 -> x0, local copies, waits for them, and re-layouts: 6.7 us -> none
    pallas_call x1 -> x2, Pallas kernels: 65.3 us -> 62.5 us  [the longest x1 60.2 us: shards(): pl.pallas_call(kernel, out_shape=shapes, in_specs=[hbm] * 5, out_specs=(h...]
where the time goes in v2:
time: 63.3 us; the launch traced here: 63.1 us
  Pallas kernels  62.5 us (99%)
  between operations  0.64 us (1%)
    pallas_call x1, Pallas kernels, shards(): pl.pallas_call(kernel, out_shape=shapes, in_specs=[hbm] * 5, out_specs=(h...  60.2 us
    pallas_call x1, Pallas kernels, shards(): pl.pallas_call(place, out_shape=shapes, in_specs=[hbm] * 3, out_specs=(hb...  2.26 us

profile of v2, /device:TPU:1, one launch (start us, length us, event | category | flops | bytes accessed | tf_op | source)
XLA Modules:
  0.0 63.1 jit_solution(6013732017370073617)
XLA Ops:
  0.6 60.2 %patch_pool.1 = (bf16[512,1024]{1,0:T(8,128)(2,1)}, f32[8,1024]{1,0:T(8,128)}, bf16[1024,256]{1,0:T(8,128)(2,1)}) custom-call(bf16[1024,256]{1,0:T(8,128)(2,1)} %h_hbm.1, s32[1,1024]{1,0:T(1,128)} %bitcast.2, bf16[2,128]{1,0:T(2,128)(2,1)} %bitcast.3, bf16[8,1024]{1,0:T(8,128)(2,1)} %w_hbm.1, bf16[512,1024]{1,0:T(8,128)(2,1)} %g_hbm.1), custom_call_target="tpu_custom_call" | custom-call | tf_op jit(solution)/shard_map/patch_pool/pallas_call | solution.py:606
  60.8 2.3 %place.1 = (bf16[512,1024]{1,0:T(8,128)(2,1)}, f32[8,1024]{1,0:T(8,128)}, bf16[1024,256]{1,0:T(8,128)(2,1)}) custom-call(bf16[512,1024]{1,0:T(8,128)(2,1)} %get-tuple-element.6.lat_in, f32[8,1024]{1,0:T(8,128)} %get-tuple-element.7.gw_in, bf16[1024,256]{1,0:T(8,128)(2,1)} %get-tuple-element.8.gb_in), custom_call_target="tpu_custom_call" | custom-call | tf_op jit(solution)/shard_map/place/pallas_call | solution.py:620

commit v3 on v2

--- a/solution.py
+++ b/solution.py
@@ -32,10 +32,6 @@
 
 def dot_nt(a, b):
     return lax.dot_general(a, b, (((1,), (1,)), ((), ())), preferred_element_type=F32)
-
-
-def dot_tn(a, b):
-    return lax.dot_general(a, b, (((0,), (0,)), ((), ())), preferred_element_type=F32)
 
 
 def split(value):
@@ -179,33 +175,15 @@
     fetched(copy_w)
     w32[...] = w_own[...].astype(F32)
     fetched(copy_st)
-    st8[...] = jnp.broadcast_to(st_own[...].astype(F32), st8.shape)
+    st8[...] = st_own[...].astype(F32)
 
     pl.semaphore_wait(barrier, 5 + 2 * (RING - 1))
 
     send(w32, w32r, W_PAIR, pair)
     send(h_hbm.at[pl.ds(rows - 16, 16)], hx.at[pl.ds(rows + 112, 16)], H_NEXT, nxt)
     send(h_hbm.at[pl.ds(0, 16)], hx.at[pl.ds(rows, 16)], H_PREV, prv)
-    send(st8.at[:, pl.ds(rows - 128, 128)], st_p, S_NEXT, nxt)
-    send(st8.at[:, pl.ds(0, 128)], st_n, S_PREV, prv)
-
-    arrived(w32r, W_PAIR)
-    w_mine, w_other = w32[...], w32r[...]
-    w16 = jnp.concatenate(
-        [jnp.where(first, w_mine, w_other), jnp.where(first, w_other, w_mine)], axis=0
-    )
-    w_half = jnp.where(first, w16[:, :512], w16[:, 512:]).astype(BF16)
-    wg[c, 0, z, y] = w_half[:, :256]
-    wg[c, 1, y, z] = w_half[:, 256:]
-
-    def lines(k):
-        send(wg.at[c, 0, z, y], wg.at[c, 0, z, y], A1A + k, dev_y(k))
-        send(wg.at[c, 1, y, z], wg.at[c, 1, y, z], A1B + k, dev_z(k))
-
-    ring(lines)
-    noted(A1A, wg.at[c, 0, z, y])
-    noted(A1B, wg.at[c, 1, y, z])
-    send(g_hbm.at[:, pair_cols], gc.at[1], G_PAIR, pair)
+    send(st8, st_p, S_NEXT, nxt)
+    send(st8, st_n, S_PREV, prv)
 
     def score(start, size):
         at = pl.ds(start, size)
@@ -217,51 +195,63 @@
         xs[at, 0:256], xs[at, 256:512] = split(w * h.astype(F32))
         xs[at, 512:768], xs[at, 768:1024] = split(w)
 
-    fetched(copy_h)
-
     def score_own(i):
         score(pl.multiple_of(i * 256, 256), 256)
 
+    fetched(copy_h)
     ring(score_own, 0, rows // 256)
+
+    arrived(w32r, W_PAIR)
+    w_mine, w_other = w32[...], w32r[...]
+    w16 = jnp.concatenate(
+        [jnp.where(first, w_mine, w_other), jnp.where(first, w_other, w_mine)], axis=0
+    )
+    w_half = jnp.where(first, w16[:, :512], w16[:, 512:]).astype(BF16)
+    wg[c, 0, z, y] = w_half[:, :256]
+    wg[c, 1, y, z] = w_half[:, 256:]
+
+    def lines(k):
+        send(wg.at[c, 0, z, y], wg.at[c, 0, z, y], A1A + k, dev_y(k))
+        send(wg.at[c, 1, y, z], wg.at[c, 1, y, z], A1B + k, dev_z(k))
+
+    ring(lines)
+    noted(A1A, wg.at[c, 0, z, y])
+    noted(A1B, wg.at[c, 1, y, z])
+    send(g_hbm.at[:, pair_cols], gc.at[1], G_PAIR, pair)
 
     r128, c128 = iota((128, 128), 0), iota((128, 128), 1)
     upper = jnp.where(r128 <= c128, 1.0, 0.0).astype(BF16)
-    lower = jnp.where(c128 <= r128, 1.0, 0.0).astype(BF16)
-    ones = jnp.ones((128, 128), BF16)
+    starts = st8[...].astype(BF16)
+    within = dot(starts, upper)
+    counts = dot(starts, jnp.ones((128, 128), BF16))
+    blocks = rows // 128
+    spread = jnp.where(iota((blocks, rows), 0) == lax.div(iota((blocks, rows), 1), 128), 1.0, 0.0)
+    within_t = lax.dot_general(
+        within.astype(BF16), spread.astype(BF16), (((0,), (0,)), ((), ())),
+        preferred_element_type=F32,
+    )
     hot_rows = hot.shape[0]
     slot_col = iota((hot_rows, 128), 0).astype(F32)
     lane = iota((128, 128), 1).astype(F32)
-    total = jnp.zeros((8, 128), F32)
+    total = jnp.zeros((1, 128), F32)
     lead8 = None
-    for k in range(rows // 128):
-        st_k = st8[:, 128 * k:128 * k + 128].astype(BF16)
-        row_id = total + dot(st_k, upper) - 1.0
+    for k in range(blocks):
+        row_id = within[k:k + 1] + total - 1.0
         row_id = jnp.where(row_id < 0.0, F32(slots), row_id)
-        hot[:, 128 * k:128 * k + 128] = jnp.where(slot_col == row_id[0:1], 1.0, 0.0).astype(BF16)
-        st_t = jnp.broadcast_to(st8[0:1, 128 * k:128 * k + 128], (128, 128)).astype(BF16)
-        col_id = dot_nt(lower, st_t) + total[0:1] - 1.0
+        hot[:, 128 * k:128 * k + 128] = jnp.where(slot_col == row_id, 1.0, 0.0).astype(BF16)
+        col_id = within_t[:, 128 * k:128 * k + 128] + total - 1.0
         if k == 0:
             lead8 = jnp.where(col_id[0:8] < 0.0, 1.0, 0.0).astype(F32)
         for j in range(slots // 128):
             hot_t[128 * k:128 * k + 128, 128 * j:128 * j + 128] = jnp.where(
                 col_id == lane + 128.0 * j, 1.0, 0.0
             ).astype(BF16)
-        total = total + dot(st_k, ones)
+        total = total + counts[k:k + 1]
     lead8 = jnp.concatenate([lead8, lead8], axis=1)
 
-    def planes(k):
-        arrived(wg.at[c, 0, z, y], A1A + k)
-        arrived(wg.at[c, 1, y, z], A1B + k)
-
-    ring(planes)
-    landed(A1A)
-    landed(A1B)
-    mine_a, mine_b = wg.at[c, 0, z], wg.at[c, 1, y]
-    for k in (2, 6, 1, 7):
-        send(mine_a, mine_a, A2A + k, dev_z(k))
-        send(mine_b, mine_b, A2B + k, dev_y(k))
-    send(mine_a, mine_a, WPA, pair)
-    send(mine_b, mine_b, WPB, pair)
+    onehot = hot[:, 0:rows]
+    sums = [dot(onehot, xs[0:rows, 256 * k:256 * k + 256]) for k in range(4)]
+    numer, denom = sums[0] + sums[1], sums[2] + sums[3]
 
     arrived(hx.at[pl.ds(rows + 112, 16)], H_NEXT)
     arrived(hx.at[pl.ds(rows, 16)], H_PREV)
@@ -270,21 +260,21 @@
     score(rows, 128)
     after = jnp.where((r128 <= c128) & (c128 < 64), 1.0, 0.0).astype(BF16)
     before = jnp.where((r128 > c128) & (c128 >= 64), 1.0, 0.0).astype(BF16)
-    starts_n = jnp.where(s == n_seq - 1, 1.0, st_n[...]).astype(BF16)
-    starts_p = jnp.where(s == 0, 1.0, st_p[...]).astype(BF16)
+    starts_n = jnp.where(s == n_seq - 1, 1.0, jnp.broadcast_to(st_n[0:1], (8, 128))).astype(BF16)
+    starts_p = jnp.where(s == 0, 1.0, jnp.broadcast_to(st_p[7:8], (8, 128))).astype(BF16)
     count = dot(starts_n, after) + dot(starts_p, before)
     halo_slot = jnp.where(iota((8, 128), 1) < 64, total - 1.0, F32(slots))
     halo_slot = jnp.where(count == 0.0, halo_slot, -9.0)
     hot[:, rows:rows + 128] = jnp.where(slot_col == halo_slot[0:1], 1.0, 0.0).astype(BF16)
 
-    onehot = hot[...]
-    denom = dot(onehot, xs[:, 512:768]) + dot(onehot, xs[:, 768:1024])
-    numer = dot(onehot, xs[:, 0:256]) + dot(onehot, xs[:, 256:512])
+    onehot = hot[:, rows:rows + 128]
+    sums = [dot(onehot, xs[rows:rows + 128, 256 * k:256 * k + 256]) for k in range(4)]
+    numer, denom = numer + sums[0] + sums[1], denom + sums[2] + sums[3]
     live = denom > 0.0
     denom = jnp.where(live, denom, 1.0)
     pooled = jnp.where(live, numer / denom, 0.0)
-    pf[0, a, 0] = pooled[:half].astype(BF16)
-    pf[0, a, 1] = pooled[half:slots].astype(BF16)
+    pf[0, a, 0] = pooled[:half].T.astype(BF16)
+    pf[0, a, 1] = pooled[half:slots].T.astype(BF16)
     send(pf.at[0, a, 0], pf.at[0, a, 0], X_UP0, up)
     send(pf.at[0, a, 1], pf.at[0, a, 1], X_DN1, dn)
     send(pf.at[0, a, 1], pf.at[0, a, 1], X_UP1, up)
@@ -302,6 +292,72 @@
     pick = jnp.where(pick & (iota((16, slots), 0) == 0), 1.0, 0.0).astype(BF16)
     gl_send[...] = dot(pick, gx[0:slots, :]).astype(BF16)
     send(gl_send, gx.at[pl.ds(slots, 16)], G_NEXT, nxt)
+
+    def grad_block(index, column):
+        value = None
+        for core in range(2):
+            for part_half in range(2):
+                term = dot(
+                    pf[core, index, part_half],
+                    gc[core, half * part_half:half * part_half + half, column:column + 256],
+                )
+                value = term if value is None else value + term
+        return value.astype(BF16)
+
+    def pair_features(step, index):
+        for part_half in range(2):
+            arrived(pf.at[1, index, part_half], PF_PAIR + 2 * step + part_half)
+
+    def grad_y(step, index):
+        if step < 3:
+            pair_features(step, index)
+        value = grad_block(index, 0)
+        for zz in range(2):
+            for yy in range(RING):
+                at = (zz * RING + yy) * 16
+                sa[yy, 2 * index + zz] = value[at:at + 16]
+        two = pl.ds(2 * index, 2)
+        base = D1A + 8 * step
+
+        def spread(k):
+            send(sa.at[y_at(k), two], ra.at[k - 1, two], base + k, dev_y(k))
+
+        ring(spread)
+        noted(base, sa.at[0, two])
+
+    def finish_y(step, index):
+        two = pl.ds(2 * index, 2)
+        base = D1A + 8 * step
+
+        def wait(k):
+            arrived(ra.at[k - 1, two], base + k)
+
+        ring(wait)
+        landed(base)
+        value = sa[y, two].astype(F32)
+        for k in range(RING - 1):
+            value = value + ra[k, two].astype(F32)
+        ta[two] = value.astype(BF16)
+        for zz in range(2):
+            k = wrap(2 * index + zz - z, RING)
+
+            @pl.when(k > 0)
+            def _():
+                send(ta.at[2 * index + zz], ua.at[k - 1], D2A + k, dev_z(k))
+
+    def grad_z(turn):
+        index = lax.rem(lax.div(z, 2) + turn, 4)
+        value = grad_block(index, 256)
+        for zz in range(2):
+            for yy in range(RING):
+                at = (zz * RING + yy) * 16
+                sb[2 * index + zz, yy] = value[at:at + 16]
+        for zz in range(2):
+            k = wrap(2 * index + zz - z, RING)
+
+            @pl.when(k > 0)
+            def _():
+                send(sb.at[2 * index + zz], rb.at[k - 1], D1B + k, dev_z(k))
 
     yv[:, 0:256], yv[:, 256:512] = split(pooled[:slots])
     yv[:, 512:768], yv[:, 768:1024] = split(denom[:slots])
@@ -328,7 +384,25 @@
     def weigh_more(i):
         weigh(pl.ds(pl.multiple_of(i * 256, 256), 256), None)
 
-    ring(weigh_more, 1, rows // 256)
+    ring(weigh_more, 1, rows // 512)
+
+    def planes(k):
+        arrived(wg.at[c, 0, z, y], A1A + k)
+        arrived(wg.at[c, 1, y, z], A1B + k)
+
+    ring(planes)
+    landed(A1A)
+    landed(A1B)
+    mine_a, mine_b = wg.at[c, 0, z], wg.at[c, 1, y]
+    for k in (2, 6, 1, 7):
+        send(mine_a, mine_a, A2A + k, dev_z(k))
+        send(mine_b, mine_b, A2B + k, dev_y(k))
+    send(mine_a, mine_a, WPA, pair)
+    send(mine_b, mine_b, WPB, pair)
+
+    fetched(copy_gc)
+    arrived(gc.at[1], G_PAIR)
+    grad_y(0, a)
 
     def whole(kind, k):
         return wg.at[c, kind, z_at(-k) if kind == 0 else y_at(-k)]
@@ -337,6 +411,14 @@
         return wg.at[c, kind, z_at(-k) if kind == 0 else y_at(-k), pl.ds(0 if lower_half else 4, 4)]
 
     kinds = ((0, A2A, dev_z, WPA), (1, A2B, dev_y, WPB))
+
+    arrived(pf.at[0, a_dn, 0], X_UP0)
+    send(pf.at[0, a_dn, 0], pf.at[0, a_dn, 0], X_UPF, up)
+    arrived(pf.at[0, a_up, 1], X_DN1)
+    send(pf.at[0, a_up, 1], pf.at[0, a_up, 1], X_DNF, dn)
+    to_pair(1, a_dn, 0)
+    to_pair(2, a_up, 1)
+    ring(weigh_more, rows // 512, rows // 256)
     for kind, base, dev, _ in kinds:
         arrived(whole(kind, 2), base + 2)
         send(whole(kind, 2), whole(kind, 2), base + 3, dev(1))
@@ -344,22 +426,26 @@
         arrived(whole(kind, 6), base + 6)
         send(whole(kind, 6), whole(kind, 6), base + 5, dev(-1))
         send(piece(kind, 6, False), piece(kind, 6, False), base, dev(-2))
-
-    arrived(pf.at[0, a_dn, 0], X_UP0)
-    send(pf.at[0, a_dn, 0], pf.at[0, a_dn, 0], X_UPF, up)
-    arrived(pf.at[0, a_up, 1], X_DN1)
-    send(pf.at[0, a_up, 1], pf.at[0, a_up, 1], X_DNF, dn)
-    to_pair(1, a_dn, 0)
-    to_pair(2, a_up, 1)
+    arrived(pf.at[0, a_dn, 1], X_UP1)
+    to_pair(1, a_dn, 1)
+    arrived(pf.at[0, a_up, 0], X_DN0)
+    to_pair(2, a_up, 0)
+    grad_y(1, a_dn)
+    grad_y(2, a_up)
+    arrived(pf.at[0, a_far, 0], X_UPF)
+    to_pair(3, a_far, 0)
+    arrived(pf.at[0, a_far, 1], X_DNF)
+    to_pair(3, a_far, 1)
     for kind, base, dev, pair_base in kinds:
         for k in (2, 6, 1, 7):
             if k in (1, 7):
                 arrived(whole(kind, k), base + k)
             send(whole(kind, k), whole(kind, k), pair_base + k, pair)
-    arrived(pf.at[0, a_dn, 1], X_UP1)
-    to_pair(1, a_dn, 1)
-    arrived(pf.at[0, a_up, 0], X_DN0)
-    to_pair(2, a_up, 0)
+    pair_features(3, a_far)
+    for turn in (2, 1, 3, 0):
+        grad_z(turn)
+    noted(D1B, sb.at[0])
+    grad_y(3, a_far)
     for kind, base, dev, pair_base in kinds:
         for k in (3, 5, 4):
             if k == 4:
@@ -368,53 +454,7 @@
             else:
                 arrived(whole(kind, k), base + k)
             send(whole(kind, k), whole(kind, k), pair_base + k, pair)
-    arrived(pf.at[0, a_far, 0], X_UPF)
-    to_pair(3, a_far, 0)
-    arrived(pf.at[0, a_far, 1], X_DNF)
-    to_pair(3, a_far, 1)
-
-    for step, index in ((0, a), (1, a_dn), (2, a_up), (3, a_far)):
-        for part_half in range(2):
-            arrived(pf.at[1, index, part_half], PF_PAIR + 2 * step + part_half)
-    fetched(copy_gc)
-    arrived(gc.at[1], G_PAIR)
-
-    def block_at(i):
-        turn = jnp.where(i == 0, 2, jnp.where(i == 1, 1, jnp.where(i == 2, 3, 0)))
-        return lax.rem(lax.div(z, 2) + turn, 4)
-
-    def grad_block(i):
-        index = block_at(i)
-        value = None
-        for core in range(2):
-            for part_half in range(2):
-                term = dot_tn(
-                    pf[core, index, part_half], gc[core, half * part_half:half * part_half + half, :]
-                )
-                value = term if value is None else value + term
-        value = value.astype(BF16)
-        for zz in range(2):
-            for yy in range(RING):
-                at = (zz * RING + yy) * 16
-                sa[yy, 2 * index + zz] = value[at:at + 16, 0:256]
-                sb[2 * index + zz, yy] = value[at:at + 16, 256:512]
-        two = pl.ds(2 * index, 2)
-
-        def spread(k):
-            send(sa.at[y_at(k), two], ra.at[k - 1, two], D1A + 8 * i + k, dev_y(k))
-
-        ring(spread)
-        for zz in range(2):
-            k = wrap(2 * index + zz - z, RING)
-
-            @pl.when(k > 0)
-            def _():
-                send(sb.at[2 * index + zz], rb.at[k - 1], D1B + k, dev_z(k))
-
-    ring(grad_block, 0, 4)
-    for i in range(4):
-        noted(D1A + 8 * i, sa.at[0, pl.ds(0, 2)])
-    noted(D1B, sb.at[0])
+    finish_y(0, a)
 
     def from_pair(k):
         arrived(wg.at[1 - c, 0, z_at(-k)], WPA + k)
@@ -457,45 +497,40 @@
     cs_dn[...] = (cr_dn[...].astype(F32) + part[2, half:half + half + 16].astype(F32)).astype(BF16)
     send(cs_dn, c_dn.at[upper_rows], C_DNS, dn)
     part[3] = partial_of(a)
+    finish_y(1, a_dn)
+    finish_y(2, a_up)
 
     def latent(part_half):
         at = pl.ds(pl.multiple_of(part_half * half, half), half)
+        values = [None] * 4
+        for index in range(4):
+            left = pf[0, index, part_half].astype(F32).T.astype(BF16)
+            for q in range(4):
+                term = dot(left, wq[q, 256 * index:256 * index + 256])
+                values[q] = term if values[q] is None else values[q] + term
         for q in range(4):
-            value = dot(pf[0, 0, part_half], wq[q, 0:256])
-            for index in range(1, 4):
-                value = value + dot(
-                    pf[0, index, part_half], wq[q, 256 * index:256 * index + 256]
-                )
-            lat_ref[at, 256 * q:256 * q + 256] = value.astype(BF16)
+            lat_ref[at, 256 * q:256 * q + 256] = values[q].astype(BF16)
 
     ring(latent, 0, 2)
     fetch(lat_ref, lat_hbm)
 
+    finish_y(3, a_far)
+    noted(D2A, ta.at[0])
+
     def reduced(k):
-        def blocks(i):
-            two = pl.ds(2 * block_at(i), 2)
-            arrived(ra.at[k - 1, two], D1A + 8 * i + k)
-
-        ring(blocks, 0, 4)
         arrived(rb.at[k - 1], D1B + k)
 
     ring(reduced)
-    for i in range(4):
-        landed(D1A + 8 * i)
     landed(D1B)
-    sum_a, sum_b = sa[y].astype(F32), sb[z].astype(F32)
+    sum_b = sb[z].astype(F32)
     for k in range(RING - 1):
-        sum_a = sum_a + ra[k].astype(F32)
         sum_b = sum_b + rb[k].astype(F32)
-    ta[...] = sum_a.astype(BF16)
     tb[...] = sum_b.astype(BF16)
 
     def reduce_more(k):
-        send(ta.at[z_at(k)], ua.at[k - 1], D2A + k, dev_z(k))
         send(tb.at[y_at(k)], ub.at[k - 1], D2B + k, dev_y(k))
 
     ring(reduce_more)
-    noted(D2A, ta.at[0])
     noted(D2B, tb.at[0])
 
     arrived(c_up.at[upper_rows], C_UPD)
@@ -549,8 +584,8 @@
 
 
 def place(lat_in, gw_in, gb_in, lat_out, gw_out, gb_out, lat, gw, gb, sem_in, sem_out):
-    parts = [(lat_in, lat, lat_out, 256 * i, 256) for i in range(lat.shape[0] // 256)]
-    parts += [(gb_in, gb, gb_out, 512 * i, 512) for i in range(gb.shape[0] // 512)]
+    parts = [(lat_in, lat, lat_out, 64 * i, 64) for i in range(lat.shape[0] // 64)]
+    parts += [(gb_in, gb, gb_out, 256 * i, 256) for i in range(gb.shape[0] // 256)]
     parts.append((gw_in, gw, gw_out, 0, 8))
     reads, writes = [], []
     for i, (src, mid, dst, start, size) in enumerate(parts):
@@ -577,8 +612,8 @@
 
     scratch = [
         buf(slots, width), buf(8, width, dtype=F32), buf(rows, feats),
-        buf(rows + 128, feats), buf(1, rows, dtype=jnp.int32), buf(2, 128),
-        buf(8, rows, dtype=F32), buf(8, 128, dtype=F32), buf(8, 128, dtype=F32),
+        buf(rows + 128, feats), buf(rows // 128, 128, dtype=jnp.int32), buf(2, 128),
+        buf(8, 128, dtype=F32), buf(8, 128, dtype=F32), buf(8, 128, dtype=F32),
         buf(8, width), buf(8, width, dtype=F32), buf(8, width, dtype=F32),
         buf(2, 2, RING, RING, 16, 256), buf(4, 1024, 256),
         buf(slots + 16, width), buf(16, width), buf(2, slots, 512),
@@ -614,7 +649,7 @@
         ),
         name="patch_pool",
     )(
-        byte_hidden, patch_start.reshape(1, rows), pool_query.reshape(2, feats // 2),
+        byte_hidden, patch_start.reshape(rows // 128, 128), pool_query.reshape(2, feats // 2),
         in_weight, latent_grad,
     )
     return pl.pallas_call(
@@ -624,7 +659,7 @@
         out_specs=(hbm, hbm, hbm),
         scratch_shapes=[
             buf(slots, width), buf(8, width, dtype=F32), buf(rows, feats),
-            pltpu.SemaphoreType.DMA((5,)), pltpu.SemaphoreType.DMA((5,)),
+            pltpu.SemaphoreType.DMA((13,)), pltpu.SemaphoreType.DMA((13,)),
         ],
         compiler_params=pltpu.CompilerParams(vmem_limit_bytes=VMEM_LIMIT),
         name="place",

time: 63.3 us -> 58 us (0.916)
  Pallas kernels: 62.5 us -> 57.2 us
    pallas_call x1, Pallas kernels: 60.2 us -> 54.9 us  [shards(): pl.pallas_call(kernel, out_shape=shapes, in_specs=[hbm] * 5, out_specs=(h...]
where the time goes in v3:
time: 58 us; the launch traced here: 57.9 us
  Pallas kernels  57.2 us (99%)
  between operations  0.64 us (1%)
    pallas_call x1, Pallas kernels, shards(): pl.pallas_call(kernel, out_shape=shapes, in_specs=[hbm] * 5, out_specs=(h...  54.9 us
    pallas_call x1, Pallas kernels, shards(): pl.pallas_call(place, out_shape=shapes, in_specs=[hbm] * 3, out_specs=(hb...  2.35 us

profile of v3, /device:TPU:1, one launch (start us, length us, event | category | flops | bytes accessed | tf_op | source)
XLA Modules:
  0.0 57.9 jit_solution(12916686689297047341)
XLA Ops:
  0.6 54.9 %patch_pool.1 = (bf16[512,1024]{1,0:T(8,128)(2,1)}, f32[8,1024]{1,0:T(8,128)}, bf16[1024,256]{1,0:T(8,128)(2,1)}) custom-call(bf16[1024,256]{1,0:T(8,128)(2,1)} %h_hbm.1, s32[8,128]{1,0:T(8,128)} %bitcast.2, bf16[2,128]{1,0:T(2,128)(2,1)} %bitcast.3, bf16[8,1024]{1,0:T(8,128)(2,1)} %w_hbm.1, bf16[512,1024]{1,0:T(8,128)(2,1)} %g_hbm.1), custom_call_target="tpu_custom_call" | custom-call | tf_op jit(solution)/shard_map/patch_pool/pallas_call | solution.py:641
  55.5 2.4 %place.1 = (bf16[512,1024]{1,0:T(8,128)(2,1)}, f32[8,1024]{1,0:T(8,128)}, bf16[1024,256]{1,0:T(8,128)(2,1)}) custom-call(bf16[512,1024]{1,0:T(8,128)(2,1)} %get-tuple-element.6.lat_in, f32[8,1024]{1,0:T(8,128)} %get-tuple-element.7.gw_in, bf16[1024,256]{1,0:T(8,128)(2,1)} %get-tuple-element.8.gb_in), custom_call_target="tpu_custom_call" | custom-call | tf_op jit(solution)/shard_map/place/pallas_call | solution.py:655

commit v4 on v3

--- a/solution.py
+++ b/solution.py
@@ -22,8 +22,8 @@
 A1A, A1B, A2A, A2B = 28, 36, 44, 52
 WPA, WPB = 60, 68
 D1A = 76
-D1B, D2A, D2B = 108, 116, 124
-SLOTS_SEM = 132
+D1B, D2A, D2B, D1F, D2F = 108, 116, 124, 132, 140
+SLOTS_SEM = 148
 
 
 def dot(a, b):
@@ -49,7 +49,7 @@
     lat_ref, gw_ref, gb_ref, hx, st_own, q_own, st8, st_n, st_p, w_own, w32, w32r, wg, wq, gx, gl_send, gc,
     hot, hot_t, xs, ws, ts, yv, share_s, diff_s, coef_s,
     pf, part, cr_up, cr_dn, cs_up, cs_dn, c_up, c_dn, zv,
-    sa, sb, ra, rb, ta, tb, ua, ub, fin_s, fin_r,
+    sa, sb, ra, rb, ta, tb, ua, ub, sf, rf, tf, uf, half_b, fin_s, fin_r,
     loc, ss, rs,
 ):
     s = lax.axis_index("seq")
@@ -345,8 +345,7 @@
             def _():
                 send(ta.at[2 * index + zz], ua.at[k - 1], D2A + k, dev_z(k))
 
-    def grad_z(turn):
-        index = lax.rem(lax.div(z, 2) + turn, 4)
+    def grad_z(index):
         value = grad_block(index, 256)
         for zz in range(2):
             for yy in range(RING):
@@ -358,6 +357,38 @@
             @pl.when(k > 0)
             def _():
                 send(sb.at[2 * index + zz], rb.at[k - 1], D1B + k, dev_z(k))
+
+    far_here = lax.div(z, 2) == a_far
+
+    def grad_far():
+        value = grad_block(a_far, 256)
+        for zz in range(2):
+            for yy in range(RING):
+                at = (zz * RING + yy) * 16
+                sf[yy, zz] = value[at:at + 16]
+
+        def spread(k):
+            send(sf.at[y_at(k)], rf.at[k - 1], D1F + k, dev_y(k))
+
+        ring(spread)
+        noted(D1F, sf.at[0])
+
+    def finish_far():
+        def wait(k):
+            arrived(rf.at[k - 1], D1F + k)
+
+        ring(wait)
+        landed(D1F)
+        value = sf[y].astype(F32)
+        for k in range(RING - 1):
+            value = value + rf[k].astype(F32)
+        tf[...] = value.astype(BF16)
+        for zz in range(2):
+            k = wrap(2 * a_far + zz - z, RING)
+
+            @pl.when(k > 0)
+            def _():
+                send(tf.at[zz], uf.at[k - 1], D2F + k, dev_z(k))
 
     yv[:, 0:256], yv[:, 256:512] = split(pooled[:slots])
     yv[:, 512:768], yv[:, 768:1024] = split(denom[:slots])
@@ -403,6 +434,7 @@
     fetched(copy_gc)
     arrived(gc.at[1], G_PAIR)
     grad_y(0, a)
+    grad_z(a)
 
     def whole(kind, k):
         return wg.at[c, kind, z_at(-k) if kind == 0 else y_at(-k)]
@@ -431,7 +463,9 @@
     arrived(pf.at[0, a_up, 0], X_DN0)
     to_pair(2, a_up, 0)
     grad_y(1, a_dn)
+    grad_z(a_dn)
     grad_y(2, a_up)
+    grad_z(a_up)
     arrived(pf.at[0, a_far, 0], X_UPF)
     to_pair(3, a_far, 0)
     arrived(pf.at[0, a_far, 1], X_DNF)
@@ -442,10 +476,8 @@
                 arrived(whole(kind, k), base + k)
             send(whole(kind, k), whole(kind, k), pair_base + k, pair)
     pair_features(3, a_far)
-    for turn in (2, 1, 3, 0):
-        grad_z(turn)
-    noted(D1B, sb.at[0])
     grad_y(3, a_far)
+    grad_far()
     for kind, base, dev, pair_base in kinds:
         for k in (3, 5, 4):
             if k == 4:
@@ -514,24 +546,25 @@
     ring(latent, 0, 2)
     fetch(lat_ref, lat_hbm)
 
+    @pl.when(jnp.logical_not(far_here))
+    def _():
+        def reduced(k):
+            arrived(rb.at[k - 1], D1B + k)
+
+        ring(reduced)
+        value = sb[z].astype(F32)
+        for k in range(RING - 1):
+            value = value + rb[k].astype(F32)
+        tb[...] = value.astype(BF16)
+
+        def reduce_more(k):
+            send(tb.at[y_at(k)], ub.at[k - 1], D2B + k, dev_y(k))
+
+        ring(reduce_more)
+
     finish_y(3, a_far)
     noted(D2A, ta.at[0])
-
-    def reduced(k):
-        arrived(rb.at[k - 1], D1B + k)
-
-    ring(reduced)
-    landed(D1B)
-    sum_b = sb[z].astype(F32)
-    for k in range(RING - 1):
-        sum_b = sum_b + rb[k].astype(F32)
-    tb[...] = sum_b.astype(BF16)
-
-    def reduce_more(k):
-        send(tb.at[y_at(k)], ub.at[k - 1], D2B + k, dev_y(k))
-
-    ring(reduce_more)
-    noted(D2B, tb.at[0])
+    finish_far()
 
     arrived(c_up.at[upper_rows], C_UPD)
     arrived(c_dn.at[lower_rows], C_DND)
@@ -560,15 +593,36 @@
 
     def reduced_more(k):
         arrived(ua.at[k - 1], D2A + k)
-        arrived(ub.at[k - 1], D2B + k)
 
     ring(reduced_more)
     landed(D2A)
-    landed(D2B)
-    sum_a, sum_b = ta[z].astype(F32), tb[y].astype(F32)
+    sum_a = ta[z].astype(F32)
     for k in range(RING - 1):
         sum_a = sum_a + ua[k].astype(F32)
-        sum_b = sum_b + ub[k].astype(F32)
+
+    @pl.when(far_here)
+    def _():
+        def wait(k):
+            arrived(uf.at[k - 1], D2F + k)
+
+        ring(wait)
+        value = tf[lax.rem(z, 2)].astype(F32)
+        for k in range(RING - 1):
+            value = value + uf[k].astype(F32)
+        half_b[...] = value
+
+    @pl.when(jnp.logical_not(far_here))
+    def _():
+        def wait(k):
+            arrived(ub.at[k - 1], D2B + k)
+
+        ring(wait)
+        value = tb[y].astype(F32)
+        for k in range(RING - 1):
+            value = value + ub[k].astype(F32)
+        half_b[...] = value
+
+    sum_b = half_b[...]
     grad_scale = 1.0 / math.sqrt(n_seq * slots)
     both = jnp.concatenate([sum_a, sum_b], axis=1) * grad_scale
     fin_s[...] = jnp.where(first, both[8:16], both[0:8])
@@ -580,6 +634,20 @@
     gw_ref[:, 512:1024] = jnp.where(first, other, mine)
     fetch(gw_ref, gw_hbm)
 
+    def left(k):
+        @pl.when(lax.div(z_at(k), 2) != a_far)
+        def _():
+            remote(sb.at[0], sb.at[0], D1B + k, pair).wait_send()
+
+        @pl.when(lax.div(z_at(k), 2) == a_far)
+        def _():
+            remote(tf.at[0], tf.at[0], D2F + k, pair).wait_send()
+
+        @pl.when(jnp.logical_not(far_here))
+        def _():
+            remote(tb.at[0], tb.at[0], D2B + k, pair).wait_send()
+
+    ring(left)
     drain()
 
 
@@ -628,6 +696,8 @@
         buf(RING - 1, RING, 16, 256), buf(RING - 1, RING, 16, 256),
         buf(RING, 16, 256), buf(RING, 16, 256),
         buf(RING - 1, 16, 256), buf(RING - 1, 16, 256),
+        buf(RING, 2, 16, 256), buf(RING - 1, 2, 16, 256),
+        buf(2, 16, 256), buf(RING - 1, 16, 256), buf(16, 256, dtype=F32),
         buf(8, 512, dtype=F32), buf(8, 512, dtype=F32),
         pltpu.SemaphoreType.DMA((9,)),
         pltpu.SemaphoreType.DMA((SLOTS_SEM,)),

time: 58 us -> 61.3 us (1.057)
  Pallas kernels: 57.2 us -> 60.5 us
    pallas_call x1, Pallas kernels: 54.9 us -> 58.2 us  [shards(): pl.pallas_call(kernel, out_shape=shapes, in_specs=[hbm] * 5, out_specs=(h...]
where the time goes in v4:
time: 61.3 us; the launch traced here: 61.2 us
  Pallas kernels  60.5 us (99%)
  between operations  0.64 us (1%)
    pallas_call x1, Pallas kernels, shards(): pl.pallas_call(kernel, out_shape=shapes, in_specs=[hbm] * 5, out_specs=(h...  58.2 us
    pallas_call x1, Pallas kernels, shards(): pl.pallas_call(place, out_shape=shapes, in_specs=[hbm] * 3, out_specs=(hb...  2.35 us

profile of v4, /device:TPU:1, one launch (start us, length us, event | category | flops | bytes accessed | tf_op | source)
XLA Modules:
  0.0 61.2 jit_solution(1781005227723931821)
XLA Ops:
  0.6 58.2 %patch_pool.1 = (bf16[512,1024]{1,0:T(8,128)(2,1)}, f32[8,1024]{1,0:T(8,128)}, bf16[1024,256]{1,0:T(8,128)(2,1)}) custom-call(bf16[1024,256]{1,0:T(8,128)(2,1)} %h_hbm.1, s32[8,128]{1,0:T(8,128)} %bitcast.2, bf16[2,128]{1,0:T(2,128)(2,1)} %bitcast.3, bf16[8,1024]{1,0:T(8,128)(2,1)} %w_hbm.1, bf16[512,1024]{1,0:T(8,128)(2,1)} %g_hbm.1), custom_call_target="tpu_custom_call" | custom-call | tf_op jit(solution)/shard_map/patch_pool/pallas_call | solution.py:711
  58.8 2.4 %place.1 = (bf16[512,1024]{1,0:T(8,128)(2,1)}, f32[8,1024]{1,0:T(8,128)}, bf16[1024,256]{1,0:T(8,128)(2,1)}) custom-call(bf16[512,1024]{1,0:T(8,128)(2,1)} %get-tuple-element.6.lat_in, f32[8,1024]{1,0:T(8,128)} %get-tuple-element.7.gw_in, bf16[1024,256]{1,0:T(8,128)(2,1)} %get-tuple-element.8.gb_in), custom_call_target="tpu_custom_call" | custom-call | tf_op jit(solution)/shard_map/place/pallas_call | solution.py:725

commit v5 on v3

--- a/solution.py
+++ b/solution.py
@@ -49,7 +49,7 @@
     lat_ref, gw_ref, gb_ref, hx, st_own, q_own, st8, st_n, st_p, w_own, w32, w32r, wg, wq, gx, gl_send, gc,
     hot, hot_t, xs, ws, ts, yv, share_s, diff_s, coef_s,
     pf, part, cr_up, cr_dn, cs_up, cs_dn, c_up, c_dn, zv,
-    sa, sb, ra, rb, ta, tb, ua, ub, fin_s, fin_r,
+    sa, sb, ra, rb, up3, up4, dn3, dn4, up_sum, dn_sum, ta, tb, ua, ub, fin_s, fin_r,
     loc, ss, rs,
 ):
     s = lax.axis_index("seq")
@@ -352,12 +352,6 @@
             for yy in range(RING):
                 at = (zz * RING + yy) * 16
                 sb[2 * index + zz, yy] = value[at:at + 16]
-        for zz in range(2):
-            k = wrap(2 * index + zz - z, RING)
-
-            @pl.when(k > 0)
-            def _():
-                send(sb.at[2 * index + zz], rb.at[k - 1], D1B + k, dev_z(k))
 
     yv[:, 0:256], yv[:, 256:512] = split(pooled[:slots])
     yv[:, 512:768], yv[:, 768:1024] = split(denom[:slots])
@@ -399,10 +393,6 @@
         send(mine_b, mine_b, A2B + k, dev_y(k))
     send(mine_a, mine_a, WPA, pair)
     send(mine_b, mine_b, WPB, pair)
-
-    fetched(copy_gc)
-    arrived(gc.at[1], G_PAIR)
-    grad_y(0, a)
 
     def whole(kind, k):
         return wg.at[c, kind, z_at(-k) if kind == 0 else y_at(-k)]
@@ -426,6 +416,10 @@
         arrived(whole(kind, 6), base + 6)
         send(whole(kind, 6), whole(kind, 6), base + 5, dev(-1))
         send(piece(kind, 6, False), piece(kind, 6, False), base, dev(-2))
+    fetched(copy_gc)
+    arrived(gc.at[1], G_PAIR)
+    grad_y(0, a)
+
     arrived(pf.at[0, a_dn, 1], X_UP1)
     to_pair(1, a_dn, 1)
     arrived(pf.at[0, a_up, 0], X_DN0)
@@ -442,9 +436,15 @@
                 arrived(whole(kind, k), base + k)
             send(whole(kind, k), whole(kind, k), pair_base + k, pair)
     pair_features(3, a_far)
-    for turn in (2, 1, 3, 0):
+    for turn in range(4):
         grad_z(turn)
-    noted(D1B, sb.at[0])
+    near, last = pl.ds(0, RING // 2), pl.ds(RING // 2, RING // 2)
+    send(sb.at[z_at(4), near], up4, D1B + 4, dev_z(2))
+    send(sb.at[z_at(4), last], dn4, D1B, dev_z(-2))
+    send(sb.at[z_at(3)], up3, D1B + 3, dev_z(1))
+    send(sb.at[z_at(5)], dn3, D1B + 5, dev_z(-1))
+    send(sb.at[z_at(1)], rb.at[0], D1B + 1, dev_z(1))
+    send(sb.at[z_at(7)], rb.at[3], D1B + 7, dev_z(-1))
     grad_y(3, a_far)
     for kind, base, dev, pair_base in kinds:
         for k in (3, 5, 4):
@@ -454,7 +454,6 @@
             else:
                 arrived(whole(kind, k), base + k)
             send(whole(kind, k), whole(kind, k), pair_base + k, pair)
-    finish_y(0, a)
 
     def from_pair(k):
         arrived(wg.at[1 - c, 0, z_at(-k)], WPA + k)
@@ -490,6 +489,19 @@
     part[2] = partial_of(a_dn)
     send(part.at[2, lower_rows], c_dn.at[lower_rows], C_DND, dn)
 
+    arrived(up4, D1B + 4)
+    arrived(up3, D1B + 3)
+    value = sb[z_at(2)].astype(F32) + up3[...].astype(F32)
+    up_sum[near] = (value[:RING // 2] + up4[...].astype(F32)).astype(BF16)
+    up_sum[last] = value[RING // 2:].astype(BF16)
+    send(up_sum, rb.at[1], D1B + 2, dev_z(2))
+    arrived(dn4, D1B)
+    arrived(dn3, D1B + 5)
+    value = sb[z_at(6)].astype(F32) + dn3[...].astype(F32)
+    dn_sum[near] = value[:RING // 2].astype(BF16)
+    dn_sum[last] = (value[RING // 2:] + dn4[...].astype(F32)).astype(BF16)
+    send(dn_sum, rb.at[2], D1B + 6, dev_z(-2))
+
     arrived(cr_up, C_UPR)
     cs_up[...] = (cr_up[...].astype(F32) + part[1, 0:half].astype(F32)).astype(BF16)
     send(cs_up, c_up.at[lower_rows], C_UPS, up)
@@ -497,6 +509,7 @@
     cs_dn[...] = (cr_dn[...].astype(F32) + part[2, half:half + half + 16].astype(F32)).astype(BF16)
     send(cs_dn, c_dn.at[upper_rows], C_DNS, dn)
     part[3] = partial_of(a)
+    finish_y(0, a)
     finish_y(1, a_dn)
     finish_y(2, a_up)
 
@@ -517,14 +530,10 @@
     finish_y(3, a_far)
     noted(D2A, ta.at[0])
 
-    def reduced(k):
-        arrived(rb.at[k - 1], D1B + k)
-
-    ring(reduced)
-    landed(D1B)
     sum_b = sb[z].astype(F32)
-    for k in range(RING - 1):
-        sum_b = sum_b + rb[k].astype(F32)
+    for i, k in enumerate((1, 2, 6, 7)):
+        arrived(rb.at[i], D1B + k)
+        sum_b = sum_b + rb[i].astype(F32)
     tb[...] = sum_b.astype(BF16)
 
     def reduce_more(k):
@@ -625,7 +634,9 @@
         buf(half, 256), buf(half + 16, 256), buf(half, 256), buf(half + 16, 256),
         buf(slots + 16, 256), buf(slots + 16, 256), buf(slots, 512),
         buf(RING, RING, 16, 256), buf(RING, RING, 16, 256),
-        buf(RING - 1, RING, 16, 256), buf(RING - 1, RING, 16, 256),
+        buf(RING - 1, RING, 16, 256), buf(4, RING, 16, 256),
+        buf(RING, 16, 256), buf(RING // 2, 16, 256), buf(RING, 16, 256), buf(RING // 2, 16, 256),
+        buf(RING, 16, 256), buf(RING, 16, 256),
         buf(RING, 16, 256), buf(RING, 16, 256),
         buf(RING - 1, 16, 256), buf(RING - 1, 16, 256),
         buf(8, 512, dtype=F32), buf(8, 512, dtype=F32),

time: 58 us -> 56.1 us (0.967)
  Pallas kernels: 57.2 us -> 55.2 us
    pallas_call x1, Pallas kernels: 54.9 us -> 52.9 us  [shards(): pl.pallas_call(kernel, out_shape=shapes, in_specs=[hbm] * 5, out_specs=(h...]
where the time goes in v5:
time: 56.1 us; the launch traced here: 55.9 us
  Pallas kernels  55.2 us (98%)
  between operations  0.64 us (1%)
    pallas_call x1, Pallas kernels, shards(): pl.pallas_call(kernel, out_shape=shapes, in_specs=[hbm] * 5, out_specs=(h...  52.9 us
    pallas_call x1, Pallas kernels, shards(): pl.pallas_call(place, out_shape=shapes, in_specs=[hbm] * 3, out_specs=(hb...  2.35 us

profile of v5, /device:TPU:1, one launch (start us, length us, event | category | flops | bytes accessed | tf_op | source)
XLA Modules:
  0.0 55.9 jit_solution(6760098508261537129)
XLA Ops:
  0.6 52.9 %patch_pool.1 = (bf16[512,1024]{1,0:T(8,128)(2,1)}, f32[8,1024]{1,0:T(8,128)}, bf16[1024,256]{1,0:T(8,128)(2,1)}) custom-call(bf16[1024,256]{1,0:T(8,128)(2,1)} %h_hbm.1, s32[8,128]{1,0:T(8,128)} %bitcast.2, bf16[2,128]{1,0:T(2,128)(2,1)} %bitcast.3, bf16[8,1024]{1,0:T(8,128)(2,1)} %w_hbm.1, bf16[512,1024]{1,0:T(8,128)(2,1)} %g_hbm.1), custom_call_target="tpu_custom_call" | custom-call | tf_op jit(solution)/shard_map/patch_pool/pallas_call | solution.py:652
  53.5 2.4 %place.1 = (bf16[512,1024]{1,0:T(8,128)(2,1)}, f32[8,1024]{1,0:T(8,128)}, bf16[1024,256]{1,0:T(8,128)(2,1)}) custom-call(bf16[512,1024]{1,0:T(8,128)(2,1)} %get-tuple-element.6.lat_in, f32[8,1024]{1,0:T(8,128)} %get-tuple-element.7.gw_in, bf16[1024,256]{1,0:T(8,128)(2,1)} %get-tuple-element.8.gb_in), custom_call_target="tpu_custom_call" | custom-call | tf_op jit(solution)/shard_map/place/pallas_call | solution.py:666

commit v6 on v5

--- a/solution.py
+++ b/solution.py
@@ -277,8 +277,6 @@
     pf[0, a, 1] = pooled[half:slots].T.astype(BF16)
     send(pf.at[0, a, 0], pf.at[0, a, 0], X_UP0, up)
     send(pf.at[0, a, 1], pf.at[0, a, 1], X_DN1, dn)
-    send(pf.at[0, a, 1], pf.at[0, a, 1], X_UP1, up)
-    send(pf.at[0, a, 0], pf.at[0, a, 0], X_DN0, dn)
 
     def to_pair(step, index, part_half):
         send(pf.at[0, index, part_half], pf.at[1, index, part_half],
@@ -388,7 +386,7 @@
     landed(A1A)
     landed(A1B)
     mine_a, mine_b = wg.at[c, 0, z], wg.at[c, 1, y]
-    for k in (2, 6, 1, 7):
+    for k in (2, 6):
         send(mine_a, mine_a, A2A + k, dev_z(k))
         send(mine_b, mine_b, A2B + k, dev_y(k))
     send(mine_a, mine_a, WPA, pair)
@@ -399,6 +397,9 @@
 
     def piece(kind, k, lower_half):
         return wg.at[c, kind, z_at(-k) if kind == 0 else y_at(-k), pl.ds(0 if lower_half else 4, 4)]
+
+    send(pf.at[0, a, 1], pf.at[0, a, 1], X_UP1, up)
+    send(pf.at[0, a, 0], pf.at[0, a, 0], X_DN0, dn)
 
     kinds = ((0, A2A, dev_z, WPA), (1, A2B, dev_y, WPB))
 
@@ -408,6 +409,9 @@
     send(pf.at[0, a_up, 1], pf.at[0, a_up, 1], X_DNF, dn)
     to_pair(1, a_dn, 0)
     to_pair(2, a_up, 1)
+    for k in (1, 7):
+        send(mine_a, mine_a, A2A + k, dev_z(k))
+        send(mine_b, mine_b, A2B + k, dev_y(k))
     ring(weigh_more, rows // 512, rows // 256)
     for kind, base, dev, _ in kinds:
         arrived(whole(kind, 2), base + 2)
@@ -443,8 +447,6 @@
     send(sb.at[z_at(4), last], dn4, D1B, dev_z(-2))
     send(sb.at[z_at(3)], up3, D1B + 3, dev_z(1))
     send(sb.at[z_at(5)], dn3, D1B + 5, dev_z(-1))
-    send(sb.at[z_at(1)], rb.at[0], D1B + 1, dev_z(1))
-    send(sb.at[z_at(7)], rb.at[3], D1B + 7, dev_z(-1))
     grad_y(3, a_far)
     for kind, base, dev, pair_base in kinds:
         for k in (3, 5, 4):
@@ -454,6 +456,9 @@
             else:
                 arrived(whole(kind, k), base + k)
             send(whole(kind, k), whole(kind, k), pair_base + k, pair)
+
+    send(sb.at[z_at(1)], rb.at[0], D1B + 1, dev_z(1))
+    send(sb.at[z_at(7)], rb.at[3], D1B + 7, dev_z(-1))
 
     def from_pair(k):
         arrived(wg.at[1 - c, 0, z_at(-k)], WPA + k)
@@ -524,8 +529,6 @@
         for q in range(4):
             lat_ref[at, 256 * q:256 * q + 256] = values[q].astype(BF16)
 
-    ring(latent, 0, 2)
-    fetch(lat_ref, lat_hbm)
 
     finish_y(3, a_far)
     noted(D2A, ta.at[0])
@@ -541,6 +544,9 @@
 
     ring(reduce_more)
     noted(D2B, tb.at[0])
+
+    ring(latent, 0, 2)
+    fetch(lat_ref, lat_hbm)
 
     arrived(c_up.at[upper_rows], C_UPD)
     arrived(c_dn.at[lower_rows], C_DND)

time: 56.1 us -> 55.2 us (0.984)
  Pallas kernels: 55.2 us -> 54.4 us
    pallas_call x1, Pallas kernels: 52.9 us -> 52 us  [shards(): pl.pallas_call(kernel, out_shape=shapes, in_specs=[hbm] * 5, out_specs=(h...]
where the time goes in v6:
time: 55.2 us; the launch traced here: 55 us
  Pallas kernels  54.4 us (99%)
  between operations  0.64 us (1%)
    pallas_call x1, Pallas kernels, shards(): pl.pallas_call(kernel, out_shape=shapes, in_specs=[hbm] * 5, out_specs=(h...  52 us
    pallas_call x1, Pallas kernels, shards(): pl.pallas_call(place, out_shape=shapes, in_specs=[hbm] * 3, out_specs=(hb...  2.35 us

profile of v6, /device:TPU:1, one launch (start us, length us, event | category | flops | bytes accessed | tf_op | source)
XLA Modules:
  0.0 55.0 jit_solution(10366650861397388571)
XLA Ops:
  0.6 52.0 %patch_pool.1 = (bf16[512,1024]{1,0:T(8,128)(2,1)}, f32[8,1024]{1,0:T(8,128)}, bf16[1024,256]{1,0:T(8,128)(2,1)}) custom-call(bf16[1024,256]{1,0:T(8,128)(2,1)} %h_hbm.1, s32[8,128]{1,0:T(8,128)} %bitcast.2, bf16[2,128]{1,0:T(2,128)(2,1)} %bitcast.3, bf16[8,1024]{1,0:T(8,128)(2,1)} %w_hbm.1, bf16[512,1024]{1,0:T(8,128)(2,1)} %g_hbm.1), custom_call_target="tpu_custom_call" | custom-call | tf_op jit(solution)/shard_map/patch_pool/pallas_call | solution.py:658
  52.7 2.4 %place.1 = (bf16[512,1024]{1,0:T(8,128)(2,1)}, f32[8,1024]{1,0:T(8,128)}, bf16[1024,256]{1,0:T(8,128)(2,1)}) custom-call(bf16[512,1024]{1,0:T(8,128)(2,1)} %get-tuple-element.6.lat_in, f32[8,1024]{1,0:T(8,128)} %get-tuple-element.7.gw_in, bf16[1024,256]{1,0:T(8,128)(2,1)} %get-tuple-element.8.gb_in), custom_call_target="tpu_custom_call" | custom-call | tf_op jit(solution)/shard_map/place/pallas_call | solution.py:672

commit v7 on v6

--- a/solution.py
+++ b/solution.py
@@ -113,6 +113,13 @@
 
         lax.fori_loop(low, high, step, 0)
 
+    def farthest_first(body):
+        def step(i):
+            turn = lax.div(i, 2)
+            body(RING // 2 + jnp.where(lax.rem(i, 2) == 0, turn, -turn))
+
+        ring(step)
+
     def noted(base, ref, low=1, high=RING):
         for k in range(low, high):
             note(base + k, ref)
@@ -154,7 +161,7 @@
         greet(dev_y(k))
         greet(dev_z(k))
 
-    ring(greet_ring)
+    farthest_first(greet_ring)
 
     own_cols = pl.ds(pl.multiple_of(c * 512, 512), 512)
     pair_cols = pl.ds(pl.multiple_of((1 - c) * 512, 512), 512)
@@ -214,7 +221,7 @@
         send(wg.at[c, 0, z, y], wg.at[c, 0, z, y], A1A + k, dev_y(k))
         send(wg.at[c, 1, y, z], wg.at[c, 1, y, z], A1B + k, dev_z(k))
 
-    ring(lines)
+    farthest_first(lines)
     noted(A1A, wg.at[c, 0, z, y])
     noted(A1B, wg.at[c, 1, y, z])
     send(g_hbm.at[:, pair_cols], gc.at[1], G_PAIR, pair)
@@ -320,7 +327,7 @@
         def spread(k):
             send(sa.at[y_at(k), two], ra.at[k - 1, two], base + k, dev_y(k))
 
-        ring(spread)
+        farthest_first(spread)
         noted(base, sa.at[0, two])
 
     def finish_y(step, index):
@@ -542,7 +549,7 @@
     def reduce_more(k):
         send(tb.at[y_at(k)], ub.at[k - 1], D2B + k, dev_y(k))
 
-    ring(reduce_more)
+    farthest_first(reduce_more)
     noted(D2B, tb.at[0])
 
     ring(latent, 0, 2)

time: 55.2 us -> 55.4 us (level)
  no operation moved by 1% of the time
where the time goes in v7:
time: 55.4 us; the launch traced here: 55.2 us
  Pallas kernels  54.6 us (99%)
  between operations  0.64 us (1%)
    pallas_call x1, Pallas kernels, shards(): pl.pallas_call(kernel, out_shape=shapes, in_specs=[hbm] * 5, out_specs=(h...  52.2 us
    pallas_call x1, Pallas kernels, shards(): pl.pallas_call(place, out_shape=shapes, in_specs=[hbm] * 3, out_specs=(hb...  2.35 us

profile of v7, /device:TPU:1, one launch (start us, length us, event | category | flops | bytes accessed | tf_op | source)
XLA Modules:
  0.0 55.2 jit_solution(16764611564007088520)
XLA Ops:
  0.6 52.2 %patch_pool.1 = (bf16[512,1024]{1,0:T(8,128)(2,1)}, f32[8,1024]{1,0:T(8,128)}, bf16[1024,256]{1,0:T(8,128)(2,1)}) custom-call(bf16[1024,256]{1,0:T(8,128)(2,1)} %h_hbm.1, s32[8,128]{1,0:T(8,128)} %bitcast.2, bf16[2,128]{1,0:T(2,128)(2,1)} %bitcast.3, bf16[8,1024]{1,0:T(8,128)(2,1)} %w_hbm.1, bf16[512,1024]{1,0:T(8,128)(2,1)} %g_hbm.1), custom_call_target="tpu_custom_call" | custom-call | tf_op jit(solution)/shard_map/patch_pool/pallas_call | solution.py:665
  52.8 2.4 %place.1 = (bf16[512,1024]{1,0:T(8,128)(2,1)}, f32[8,1024]{1,0:T(8,128)}, bf16[1024,256]{1,0:T(8,128)(2,1)}) custom-call(bf16[512,1024]{1,0:T(8,128)(2,1)} %get-tuple-element.6.lat_in, f32[8,1024]{1,0:T(8,128)} %get-tuple-element.7.gw_in, bf16[1024,256]{1,0:T(8,128)(2,1)} %get-tuple-element.8.gb_in), custom_call_target="tpu_custom_call" | custom-call | tf_op jit(solution)/shard_map/place/pallas_call | solution.py:679
